TPU v7x, 512 devices: a whole 4x8x8 slice. The times are simulated.
512 devices in a mesh: px: 16 (over y, core), py: 32 (over z, x).
Axes of the slice: x: 4, y: 8, z: 8, core: 2. Of those that a mesh axis runs over, the one named last changes fastest.
Arguments:
- right_side: float32 [16, 32, 16512], P('px', 'py')
- geometry: float32 [16, 32, 3, 48, 512], P('px', 'py'), may hold values from 0.3 to 3
- shift: float32 [16, 32, 48], P('px', 'py'), may hold values from 4 to 40
- node_order: int32 [16, 32, 48, 512], P('px', 'py'), may hold values from 0 to 511, as said below
- elem_counts: int32 [16, 32], P('px', 'py'), may hold values from 18 to 48, as said below
- share_lists: int32 [16, 32, 4, 1536], P('px', 'py'), may hold values from 0 to 1280, as said below
Outputs:
- solution_field: float32 [16, 32, 16512], P('px', 'py')
- residual: float32 [16, 32, 16512], P('px', 'py')
Inputs may be any that keep to these rules, and one draw needn't show every extreme that they name: Every row node_order[i, j, e, :] is a permutation of 0 to 511. `elem_counts`: some partition has exactly 48 live elements. `share_lists`: the used entries of each part of a list come first and are distinct; the k-th used face entry of a partition's list toward a neighbour and of the neighbour's list back name the same node, and the k-th node of a crossing is the same node in the four partitions around it, in every list that names that crossing. Partitions at the grid's ends have no used entries toward missing neighbours. Some face has 1280 shared nodes and some crossing 128.
All inputs are finite; a program needn't handle non-finite values.
Results may differ from a plain program's by a relative error of at most 0.0003.
Values sent between devices are 32-bit elements; how exact they have to be, the bound alone decides.
A program may use at most 64 MiB of HBM per device.

v0:
```python
import jax
import jax.numpy as jnp
import numpy as np
from jax import lax
from jax.sharding import PartitionSpec as P

STRIDE = 344
ITERS = 2
FACE = 1280
DIAG = 128


def padded(cells, sides, width):
    for axis, dim in sides:
        count = lax.axis_size(axis)
        ends = count - 1
        head = lax.slice_in_dim(cells, 0, width, axis=dim)
        tail = lax.slice_in_dim(cells, cells.shape[dim] - width, cells.shape[dim], axis=dim)
        cells = jnp.concatenate(
            [
                lax.ppermute(tail, axis, [(i, (i + 1) % count) for i in range(ends)]),
                cells,
                lax.ppermute(head, axis, [((i + 1) % count, i) for i in range(ends)]),
            ],
            axis=dim,
        )
    return cells


def gll_derivative():
    degree = 7
    points = np.array(
        [
            -1.0,
            -0.8717401485096066,
            -0.5917001814331423,
            -0.2092992179024789,
            0.2092992179024789,
            0.5917001814331423,
            0.8717401485096066,
            1.0,
        ]
    )
    before = np.ones(8)
    current = points * 1.0
    for order in range(1, degree):
        following = ((2 * order + 1) * points * current - order * before) / (order + 1)
        before = current
        current = following
    same = np.arange(8)[:, None] == np.arange(8)[None, :]
    spacing = np.where(same, 1.0, points[:, None] - points[None, :])
    matrix = np.where(same, 0.0, current[:, None] / (current[None, :] * spacing))
    corner = np.array([-14.0, 0.0, 0.0, 0.0, 0.0, 0.0, 0.0, 14.0])
    return matrix + np.where(same, corner[:, None], 0.0)


def direction_tables():
    deriv = gll_derivative()
    first_table = np.kron(deriv, np.eye(64))
    second_table = np.kron(np.eye(2), np.kron(deriv, np.eye(8)))
    third_table = np.kron(np.eye(16), deriv)
    return (first_table, second_table, third_table)


def node_index_of(order_dev, live):
    row_ids = jnp.arange(order_dev.shape[0], dtype=jnp.int32)[:, None]
    return (row_ids * STRIDE + order_dev) % (live * STRIDE)


def element_terms(values_in, node_index, geo_dev, shift_vals, alive):
    first_np, second_np, third_np = direction_tables()
    first_table = jnp.asarray(first_np, dtype=jnp.float32)
    second_table = jnp.asarray(second_np, dtype=jnp.float32)
    third_table = jnp.asarray(third_np, dtype=jnp.float32)
    exact = lax.Precision.HIGHEST
    rows = node_index.shape[0]
    gathered = jnp.take(values_in, node_index, axis=0)
    narrow = gathered.reshape(rows * 4, 128)
    grad_r = jnp.dot(gathered, first_table.T, precision=exact)
    grad_s = jnp.dot(narrow, second_table.T, precision=exact).reshape(rows, 512)
    grad_t = jnp.dot(narrow, third_table.T, precision=exact).reshape(rows, 512)
    result = jnp.dot(geo_dev[0] * grad_r, first_table, precision=exact)
    back_s = jnp.dot((geo_dev[1] * grad_s).reshape(rows * 4, 128), second_table, precision=exact)
    back_t = jnp.dot((geo_dev[2] * grad_t).reshape(rows * 4, 128), third_table, precision=exact)
    result = result + back_s.reshape(rows, 512) + back_t.reshape(rows, 512)
    result = result + shift_vals[:, None] * gathered
    return result * alive[:, None]


def list_targets(lists_dev, nodes_total):
    position = jnp.arange(lists_dev.shape[1], dtype=jnp.int32)[None, :]
    is_face = position < FACE
    is_lower = (position >= FACE) & (position < FACE + DIAG)
    face_base = jnp.array([0, 1, 2, 3], jnp.int32)[:, None] * FACE
    lower_base = 4 * FACE + jnp.array([1, 3, 2, 3], jnp.int32)[:, None] * DIAG
    upper_base = 4 * FACE + jnp.array([0, 2, 0, 1], jnp.int32)[:, None] * DIAG
    region_base = jnp.where(is_face, face_base, jnp.where(is_lower, lower_base, upper_base))
    region_size = jnp.where(is_face, FACE, DIAG)
    is_valid = lists_dev < region_size
    targets = jnp.where(is_valid, region_base + lists_dev, nodes_total)
    weights = jnp.where(is_valid, jnp.where(is_face, 1.0, 1.5), 0.0).astype(jnp.float32)
    return (targets, weights)


def assemble(partial_value, targets):
    width_list = targets.shape[1]
    sent = jnp.take(partial_value, targets, axis=0, mode="fill", fill_value=0.0)
    got_x = padded(jnp.stack([sent[1], sent[0]]), (("px", 0),), 1)
    from_below = got_x[0]
    from_above = got_x[3]
    summed = partial_value.at[targets[1]].add(from_below, mode="drop")
    summed = summed.at[targets[0]].add(from_above, mode="drop")
    down_row = jnp.concatenate(
        [sent[3], from_below[FACE : FACE + DIAG], from_above[FACE : FACE + DIAG]]
    )
    up_row = jnp.concatenate([sent[2], from_below[FACE + DIAG :], from_above[FACE + DIAG :]])
    got_y = padded(jnp.stack([down_row, up_row]), (("py", 0),), 1)
    below_y = got_y[0]
    above_y = got_y[3]
    summed = summed.at[targets[3]].add(below_y[:width_list], mode="drop")
    summed = summed.at[targets[3, FACE:]].add(below_y[width_list:], mode="drop")
    summed = summed.at[targets[2]].add(above_y[:width_list], mode="drop")
    summed = summed.at[targets[2, FACE:]].add(above_y[width_list:], mode="drop")
    return summed


def body(right_side, geometry, shift, node_order, elem_counts, share_lists):
    live = elem_counts[0, 0]
    rhs_local = right_side[0, 0]
    nodes_total = rhs_local.shape[0]
    geo_dev = geometry[0, 0]
    shift_dev = shift[0, 0]
    order_dev = node_order[0, 0]
    elem_slots = order_dev.shape[0]
    node_index = node_index_of(order_dev, live)
    targets, weights = list_targets(share_lists[0, 0], nodes_total)
    multiplicity = 1.0 + jnp.zeros((nodes_total,), jnp.float32).at[targets.reshape(-1)].add(
        weights.reshape(-1), mode="drop"
    )
    inverse = 1.0 / multiplicity

    def squares(vector):
        return lax.psum(jnp.sum(vector * vector * inverse), ("px", "py"))

    rhs_live = jnp.where(jnp.arange(nodes_total, dtype=jnp.int32) < live * STRIDE, rhs_local, 0.0)
    residual = assemble(rhs_live, targets)
    solution_field = jnp.zeros_like(residual)
    direction = residual
    norm_now = squares(residual)
    for step in range(ITERS):
        alive = (jnp.arange(elem_slots, dtype=jnp.int32) < live).astype(jnp.float32)
        terms = element_terms(direction, node_index, geo_dev, shift_dev, alive)
        image = assemble(
            jnp.zeros((nodes_total,), jnp.float32)
            .at[node_index.reshape(-1)]
            .add(terms.reshape(-1)),
            targets,
        )
        alpha = norm_now / lax.psum(jnp.sum(direction * image * inverse), ("px", "py"))
        solution_field = solution_field + alpha * direction
        residual = residual - alpha * image
        norm_next = squares(residual)
        direction = residual + norm_next / norm_now * direction
        norm_now = norm_next
    return (solution_field[None, None], residual[None, None])


def solution(mesh):
    return jax.shard_map(
        body,
        mesh=mesh,
        in_specs=(
            P("px", "py", None),
            P("px", "py", None, None, None),
            P("px", "py", None),
            P("px", "py", None, None),
            P("px", "py"),
            P("px", "py", None, None),
        ),
        out_specs=(P("px", "py", None), P("px", "py", None)),
        check_vma=False,
    )
```

profile of v0, /device:TPU:1, one launch (start us, length us, event | category | flops | bytes accessed | tf_op | source)
XLA Modules:
  0.0 1236.9 jit_solution(3009972567286199783)
XLA Ops:
  3.9 34.3 %gather_fusion = f32[6144]{0:T(1024)S(1)} fusion(f32[16512]{0:T(1024)S(1)} %fusion.9, s32[6144]{0:T(1024)S(1)} %broadcast_clamp_fusion.1), kind=kCustom, calls=%fused_computation.clone | custom fusion | bytes 73728 | tf_op jit(solution)/shard_map/jit(_take)/gather | solution.py:107
  38.3 4.6 collective-permute-start
  42.9 5.5 collective-permute-start.1
  50.0 7.6 compare_select_fusion
  60.6 10.2 scatter_fusion
  70.8 10.3 scatter_fusion.1
  81.2 11.2 scatter_fusion.2
  93.1 2.3 scatter_fusion.3
  95.5 9.5 scatter_fusion.4
  105.7 2.5 scatter_fusion.5
  108.2 135.5 %gather_fusion.1 = f32[24576]{0:T(1024)S(1)} fusion(f32[16512]{0:T(1024)S(1)} %scatter_fusion.5, s32[24576]{0:T(1024)S(1)} %broadcast_clamp_fusion), kind=kCustom, calls=%fused_computation.1.clone | custom fusion | bytes 294912 | tf_op jit(solution)/shard_map/jit(_take)/gather | solution.py:77
  249.4 156.8 %scatter_custom_fusion.7 = f32[16512]{0:T(1024)S(1)} fusion(s32[24576]{0:T(1024)S(1)} %bitcast.155, f32[24576]{0:T(1024)S(1)} %bitcast.151, f32[]{:T(128)} %constant.10.clone.1), kind=kCustom, calls=%fused_computation.75 | custom fusion | flops 24576 | bytes 66052 | tf_op jit(solution)/shard_map/scatter-add | solution.py:156
  406.2 34.3 %gather_fusion.2 = f32[6144]{0:T(1024)S(1)} fusion(f32[16512]{0:T(1024)S(1)} %scatter_custom_fusion.7, s32[6144]{0:T(1024)S(1)} %broadcast_clamp_fusion.1), kind=kCustom, calls=%fused_computation.2.clone | custom fusion | bytes 73728 | tf_op jit(solution)/shard_map/jit(_take)/gather | solution.py:107
  442.9 39.0 %scatter_custom_fusion.6 = f32[16512]{0:T(1024)S(1)} fusion(s32[6144]{0:T(1024)S(1)} %bitcast.157, f32[6144]{0:T(1024)S(1)} %compare_select_fusion.9, f32[]{:T(128)} %constant.40.clone.1), kind=kCustom, calls=%fused_computation.71 | custom fusion | flops 6144 | bytes 66052 | tf_op jit(solution)/shard_map/scatter-add | solution.py:137
  481.8 3.2 collective-permute-start.4
  487.2 10.0 scatter_fusion.6
  498.6 10.3 scatter_fusion.7
  508.9 11.2 scatter_fusion.8
  520.8 2.3 scatter_fusion.9
  523.2 9.9 scatter_fusion.10
  536.8 109.7 %all-reduce = (f32[]{:T(128)}, f32[]{:T(128)}) all-reduce(f32[]{:T(128)} %get-tuple-element.5, f32[]{:T(128)} %get-tuple-element.4), channel_id=1, replica_groups=mesh['px'=16,'py'=32] {'px','py'}, use_global_device_ids=true, to_apply=%region_8.10 | all-reduce | flops 2 | bytes 16 | tf_op jit(solution)/shard_map/psum | solution.py:143
  648.4 95.0 %psum.30 = f32[]{:T(128)} all-reduce(f32[]{:T(128)} %multiply_reduce_fusion.1), channel_id=1, replica_groups=mesh['px'=16,'py'=32] {'px','py'}, use_global_device_ids=true, to_apply=%region_19.22 | all-reduce | flops 1 | bytes 8 | tf_op jit(solution)/shard_map/psum | solution.py:143
  744.8 135.5 %gather_fusion.3 = f32[24576]{0:T(1024)S(1)} fusion(f32[16512]{0:T(1024)S(1)} %multiply_add_fusion.1, s32[24576]{0:T(1024)S(1)} %broadcast_clamp_fusion), kind=kCustom, calls=%fused_computation.4.clone | custom fusion | bytes 294912 | tf_op jit(solution)/shard_map/jit(_take)/gather | solution.py:77
  884.5 156.8 %scatter_custom_fusion.14 = f32[16512]{0:T(1024)S(1)} fusion(s32[24576]{0:T(1024)S(1)} %bitcast.156, f32[24576]{0:T(1024)S(1)} %bitcast.150, f32[]{:T(128)} %constant.10.clone.1), kind=kCustom, calls=%fused_computation.73 | custom fusion | flops 24576 | bytes 66052 | tf_op jit(solution)/shard_map/scatter-add | solution.py:156
  1041.3 34.3 %gather_fusion.4 = f32[6144]{0:T(1024)S(1)} fusion(f32[16512]{0:T(1024)S(1)} %scatter_custom_fusion.14, s32[6144]{0:T(1024)S(1)} %broadcast_clamp_fusion.1), kind=kCustom, calls=%fused_computation.3.clone | custom fusion | bytes 73728 | tf_op jit(solution)/shard_map/jit(_take)/gather | solution.py:107
  1075.7 2.5 collective-permute-start.9
  1078.2 4.3 collective-permute-start.8
  1085.5 10.0 scatter_fusion.12
  1096.9 10.5 scatter_fusion.13
  1107.5 11.2 scatter_fusion.14
  1121.7 9.5 scatter_fusion.16
  1134.9 99.1 %psum.31 = f32[]{:T(128)} all-reduce(f32[]{:T(128)} %multiply_reduce_fusion), channel_id=1, replica_groups=mesh['px'=16,'py'=32] {'px','py'}, use_global_device_ids=true, to_apply=%region_28.31 | all-reduce | flops 1 | bytes 8 | tf_op jit(solution)/shard_map/psum | solution.py:159
  (167 shorter events, 40.9 us)
Async XLA Ops:
  1.3 0.7 copy-start.15
  2.8 0.9 copy-start.6
  3.9 44.6 %copy-start.5 = (s32[1,1,4,1536]{3,2,1,0:T(4,128)S(1)}, s32[1,1,4,1536]{3,2,1,0:T(4,128)}, u32[]{:S(2)}) copy-start(s32[1,1,4,1536]{3,2,1,0:T(4,128)} %param.24) | copy-start | bytes 73732
  38.2 10.3 copy-start.1
  38.3 19.6 %collective-permute-start = (f32[1,1536]{1,0:T(1,128)S(1)}, f32[1,1536]{1,0:T(1,128)S(1)}, u32[]{:S(2)}, u32[]{:S(2)}) collective-permute-start(f32[1,1536]{1,0:T(1,128)S(1)} %get-tuple-element.33), channel_id=1, source_target_pairs={{0,32},{32,64},{64,96},{96,128},{128,160},{160,192},{192,224},{224... | collective-permute-start | bytes 18440 | tf_op jit(solution)/shard_map/ppermute | solution.py:21
  42.9 15.0 %collective-permute-start.1 = (f32[1,1536]{1,0:T(1,128)S(1)}, f32[1,1536]{1,0:T(1,128)S(1)}, u32[]{:S(2)}, u32[]{:S(2)}) collective-permute-start(f32[1,1536]{1,0:T(1,128)S(1)} %get-tuple-element.32), channel_id=1, source_target_pairs={{32,0},{64,32},{96,64},{128,96},{160,128},{192,160},{224,192},{256... | collective-permute-start | bytes 18440 | tf_op jit(solution)/shard_map/ppermute | solution.py:23
  48.7 1.2 copy-start.4
  57.9 23.2 %collective-permute-start.2 = (f32[1,1792]{1,0:T(1,128)S(1)}, f32[1,1792]{1,0:T(1,128)S(1)}, u32[]{:S(2)}, u32[]{:S(2)}) collective-permute-start(f32[1,1792]{1,0:T(1,128)S(1)} %stack.18), channel_id=1, source_target_pairs={{0,1},{1,2},{2,3},{3,4},{4,5},{5,6},{6,7},{7,8},{8,9},{9,10},{10,1... | collective-permute-start | bytes 21512 | tf_op jit(solution)/shard_map/ppermute | solution.py:21
  59.3 36.2 %collective-permute-start.3 = (f32[1,1792]{1,0:T(1,128)S(1)}, f32[1,1792]{1,0:T(1,128)S(1)}, u32[]{:S(2)}, u32[]{:S(2)}) collective-permute-start(f32[1,1792]{1,0:T(1,128)S(1)} %stack.19), channel_id=1, source_target_pairs={{1,0},{2,1},{3,2},{4,3},{5,4},{6,5},{7,6},{8,7},{9,8},{10,9},{11,1... | collective-permute-start | bytes 21512 | tf_op jit(solution)/shard_map/ppermute | solution.py:23
  81.2 11.2 copy-start.9
  92.4 0.7 slice-start.2
  95.4 9.5 copy-start.8
  105.0 0.7 slice-start.1
  108.2 136.7 %copy-start.3 = (f32[128,128]{1,0:T(8,128)S(1)}, f32[128,128]{1,0:T(8,128)}, u32[]{:S(2)}) copy-start(f32[128,128]{1,0:T(8,128)} %constant.47.clone) | copy-start | bytes 196612
  243.8 3.0 copy-start
  245.4 0.8 copy-start.2
  440.6 44.5 %collective-permute-start.5 = (f32[1,1536]{1,0:T(1,128)S(1)}, f32[1,1536]{1,0:T(1,128)S(1)}, u32[]{:S(2)}, u32[]{:S(2)}) collective-permute-start(f32[1,1536]{1,0:T(1,128)S(1)} %get-tuple-element.28), channel_id=1, source_target_pairs={{32,0},{64,32},{96,64},{128,96},{160,128},{192,160},{224,192},{256... | collective-permute-start | bytes 18440 | tf_op jit(solution)/shard_map/ppermute | solution.py:23
  481.8 4.0 collective-permute-start.4
  485.8 23.1 %collective-permute-start.6 = (f32[1,1792]{1,0:T(1,128)S(1)}, f32[1,1792]{1,0:T(1,128)S(1)}, u32[]{:S(2)}, u32[]{:S(2)}) collective-permute-start(f32[1,1792]{1,0:T(1,128)S(1)} %stack.20), channel_id=1, source_target_pairs={{0,1},{1,2},{2,3},{3,4},{4,5},{5,6},{6,7},{7,8},{8,9},{9,10},{10,1... | collective-permute-start | bytes 21512 | tf_op jit(solution)/shard_map/ppermute | solution.py:21
  497.2 25.9 %collective-permute-start.7 = (f32[1,1792]{1,0:T(1,128)S(1)}, f32[1,1792]{1,0:T(1,128)S(1)}, u32[]{:S(2)}, u32[]{:S(2)}) collective-permute-start(f32[1,1792]{1,0:T(1,128)S(1)} %stack.21), channel_id=1, source_target_pairs={{1,0},{2,1},{3,2},{4,3},{5,4},{6,5},{7,6},{8,7},{9,8},{10,9},{11,1... | collective-permute-start | bytes 21512 | tf_op jit(solution)/shard_map/ppermute | solution.py:23
  508.9 11.2 copy-start.10
  520.1 0.7 slice-start.3
  523.2 9.9 copy-start.12
  533.1 0.7 slice-start.5
  1075.7 6.8 collective-permute-start.9
  1078.2 5.1 collective-permute-start.8
  1083.3 24.1 %collective-permute-start.10 = (f32[1,1792]{1,0:T(1,128)S(1)}, f32[1,1792]{1,0:T(1,128)S(1)}, u32[]{:S(2)}, u32[]{:S(2)}) collective-permute-start(f32[1,1792]{1,0:T(1,128)S(1)} %stack.22), channel_id=1, source_target_pairs={{0,1},{1,2},{2,3},{3,4},{4,5},{5,6},{6,7},{7,8},{8,9},{9,10},{10,1... | collective-permute-start | bytes 21512 | tf_op jit(solution)/shard_map/ppermute | solution.py:21
  1095.6 26.1 %collective-permute-start.11 = (f32[1,1792]{1,0:T(1,128)S(1)}, f32[1,1792]{1,0:T(1,128)S(1)}, u32[]{:S(2)}, u32[]{:S(2)}) collective-permute-start(f32[1,1792]{1,0:T(1,128)S(1)} %stack.23), channel_id=1, source_target_pairs={{1,0},{2,1},{3,2},{4,3},{5,4},{6,5},{7,6},{8,7},{9,8},{10,9},{11,1... | collective-permute-start | bytes 21512 | tf_op jit(solution)/shard_map/ppermute | solution.py:23
  1107.4 11.2 copy-start.7
  1118.6 0.7 slice-start
  1121.7 9.5 copy-start.11
  1131.2 0.7 slice-start.4
  (2 other events, 1.3 us)
where the time goes:
time: 1250 us; the launch traced here: 1240 us
  other arithmetic  505 us (40%)
  local copies, waits for them, and re-layouts  383 us (31%)
  blocking collectives  304 us (24%)
  starting transfers between devices  30.9 us (2%)
    scatter-add x2, other arithmetic, body(): image = assemble(jnp.zeros((nodes_total,), jnp.float32).at[node_index.res...  314 us
    gather x4, local copies, waits for them, and re-layouts, element_terms(): gathered = jnp.take(values_in, node_index, axis=0)  271 us
    psum x2, blocking collectives, squares(): return lax.psum(jnp.sum(vector * vector * inverse), ('px', 'py'))  205 us
    gather x6, local copies, waits for them, and re-layouts, assemble(): sent = jnp.take(partial_value, targets, axis=0, mode='fill', fill_value=0.0)  103 us
    psum x1, blocking collectives, body(): lax.psum(jnp.sum(direction * image * inverse), ('px', 'py'))  99.1 us
    scatter-add x1, other arithmetic, body(): jnp.zeros((nodes_total,), jnp.float32).at[targets.reshape(-1)]  39 us
    scatter-add x3, other arithmetic, assemble(): summed = summed.at[targets[3]].add(below_y[:width_list], mode='drop')  33.5 us
    scatter-add x3, other arithmetic, assemble(): summed = summed.at[targets[0]].add(from_above, mode='drop')  31.2 us
  transfers between devices with their start and end apart: 12, of which 2 were waited for; matrix products, arithmetic and copies ran while one was open for 12% of the time, Pallas kernels for 0%

commit v1 on v0

v1 whole, which is shorter than its diff:
```python
import functools

import jax
import jax.numpy as jnp
import numpy as np
from jax import lax
from jax.experimental import pallas as pl
from jax.experimental.pallas import tpu as pltpu
from jax.sharding import PartitionSpec as P

STRIDE = 344
FACE = 1280
DIAG = 128
ELEMS = 48
LANES = 128
ROWS = 129
PAD = 136
FACE_ROWS = FACE // LANES
TURN = 80
ROW_OF = [e * STRIDE // LANES for e in range(ELEMS)]
LOWER = (1, 3, 2, 3)
UPPER = (0, 2, 0, 1)
FACE_STEPS = ((1, 0), (-1, 0), (0, 1), (0, -1))
DIAG_STEPS = ((1, 1), (1, -1), (-1, 1), (-1, -1))
DIAG_LIST = (0, 0, 1, 1)


def gll_derivative():
    degree = 7
    points = np.array(
        [
            -1.0,
            -0.8717401485096066,
            -0.5917001814331423,
            -0.2092992179024789,
            0.2092992179024789,
            0.5917001814331423,
            0.8717401485096066,
            1.0,
        ]
    )
    before = np.ones(8)
    current = points * 1.0
    for order in range(1, degree):
        following = ((2 * order + 1) * points * current - order * before) / (order + 1)
        before = current
        current = following
    same = np.arange(8)[:, None] == np.arange(8)[None, :]
    spacing = np.where(same, 1.0, points[:, None] - points[None, :])
    matrix = np.where(same, 0.0, current[:, None] / (current[None, :] * spacing))
    corner = np.array([-14.0, 0.0, 0.0, 0.0, 0.0, 0.0, 0.0, 14.0])
    return matrix + np.where(same, corner[:, None], 0.0)


def tables():
    deriv = gll_derivative()
    half = np.arange(LANES) // 64

    def lanes_of(matrix):
        rows = []
        for out in range(4):
            for src in range(4):
                rows.append(matrix[2 * out + half, 2 * src + half])
                rows.append(matrix[2 * out + half, 2 * src + 1 - half])
        return np.stack(rows)

    coef = np.concatenate([lanes_of(deriv), lanes_of(deriv.T)])
    second = np.kron(np.eye(2), np.kron(deriv, np.eye(8)))
    third = np.kron(np.eye(16), deriv)
    ahead = np.concatenate([second.T, third.T], axis=1)
    back = np.concatenate([second, third], axis=0)
    return tuple(np.asarray(t, np.float32) for t in (coef, ahead, back))


def take_lanes(values, lanes):
    return jnp.take_along_axis(values, lanes, axis=1, mode="promise_in_bounds")


def pick(sources, index):
    high = index >> 7
    lanes = index & 127
    total = None
    for j, source in enumerate(sources):
        term = jnp.where(high == j, take_lanes(source, lanes), 0.0)
        total = term if total is None else total + term
    return total


def eight(row):
    return jnp.broadcast_to(row, (8, row.shape[1]))


def iota(shape, dim):
    return lax.broadcasted_iota(jnp.int32, shape, dim)


def one_hot_lanes(low):
    return jnp.where(low == iota((LANES, low.shape[1]), 0), 1.0, 0.0).astype(jnp.bfloat16)


def over_lanes(left, right):
    return lax.dot_general(
        left, right, (((1,), (1,)), ((), ())), preferred_element_type=jnp.float32
    )


def inverse_rows(high, low, groups):
    count = high.shape[1]
    number = iota((groups, count), 1) + 1
    hit = high == iota((groups, count), 0)
    tens = jnp.where(hit, number >> 4, 0).astype(jnp.float32)
    ones = jnp.where(hit, number & 15, 0).astype(jnp.float32)
    left = jnp.concatenate([tens, ones], axis=0).astype(jnp.bfloat16)
    found = over_lanes(left, one_hot_lanes(low))
    return (16.0 * found[:groups] + found[groups:]).astype(jnp.int32) - 1


def kernel(
    n_px,
    n_py,
    rhs_ref,
    geo_ref,
    shift_ref,
    order_ref,
    count_ref,
    lists_ref,
    coef_ref,
    ahead_ref,
    back_ref,
    sol_ref,
    res_ref,
    resid,
    image,
    second,
    part_w,
    windows,
    spread,
    sums,
    elem_inv,
    face_inv,
    cross_inv,
    wrap_inv,
    inv_mult,
    cross_src,
    send,
    recv,
    recv_diag,
    red,
    send_sem,
    recv_sem,
):
    px = lax.axis_index("px")
    py = lax.axis_index("py")

    def moved(step_x, step_y):
        return (lax.rem(px + step_x + n_px, n_px), lax.rem(py + step_y + n_py, n_py))

    low_py = 4 if n_py >= 16 else 2
    phases = (
        ((1, 2), (1, low_py)),
        ((2, n_px // 2), (1, 1)),
        ((1, 1), (low_py, n_py // low_py)),
    )

    def place(phase):
        (stride_x, size_x), (stride_y, size_y) = phase
        at_x = lax.rem(px // stride_x, size_x)
        at_y = lax.rem(py // stride_y, size_y)
        return at_x, at_y

    def partners(phase):
        (stride_x, size_x), (stride_y, size_y) = phase
        at_x, at_y = place(phase)
        found = []
        for dx in range(size_x):
            for dy in range(size_y):
                if dx or dy:
                    to_x = lax.rem(at_x + dx, size_x)
                    to_y = lax.rem(at_y + dy, size_y)
                    found.append((px + (to_x - at_x) * stride_x, py + (to_y - at_y) * stride_y))
        return found

    everyone = [moved(*step) for step in FACE_STEPS + DIAG_STEPS]
    for phase in phases:
        everyone += partners(phase)
    barrier = pltpu.get_barrier_semaphore()
    for other in everyone:
        pl.semaphore_signal(
            barrier, inc=1, device_id=other, device_id_type=pl.DeviceIdType.MESH
        )

    copies = []

    def start_copy(src, dst, other):
        number = len(copies)
        copy = pltpu.make_async_remote_copy(
            src_ref=src,
            dst_ref=dst,
            send_sem=send_sem.at[number],
            recv_sem=recv_sem.at[number],
            device_id=other,
            device_id_type=pl.DeviceIdType.MESH,
        )
        copy.start()
        copies.append(copy)
        return copy

    def start_exchange(turn):
        started = []
        for f, step in enumerate(FACE_STEPS):
            started.append(
                start_copy(
                    send.at[pl.ds(TURN * turn + 16 * f, 16)],
                    recv.at[pl.ds(TURN * turn + 16 * (f ^ 1), 16)],
                    moved(*step),
                )
            )
        for d, step in enumerate(DIAG_STEPS):
            started.append(
                start_copy(
                    send.at[pl.ds(TURN * turn + 16 * DIAG_LIST[d] + 8, 8)],
                    recv_diag.at[pl.ds(32 * turn + 8 * (3 - d), 8)],
                    moved(*step),
                )
            )
        return started

    def start_sum(turn, number, block):
        phase = phases[number]
        at_x, at_y = place(phase)
        mine = at_x * phase[1][1] + at_y
        red[turn, number, pl.ds(mine, 1)] = block[None]
        return [
            start_copy(red.at[turn, number, mine], red.at[turn, number, mine], other)
            for other in partners(phase)
        ]

    def end_sum(turn, number, started):
        for copy in started:
            copy.wait_recv()
        size = phases[number][0][1] * phases[number][1][1]
        total = red[turn, number, 0]
        for slot in range(1, size):
            total = total + red[turn, number, slot]
        return total

    live = count_ref[...]

    def fill_send(turn, source):
        for i in range(FACE_ROWS):
            index = lists_ref[:, i * LANES : (i + 1) * LANES]
            found = pick(
                [source[pl.ds(j, 4, stride=FACE_ROWS), :] for j in range(FACE_ROWS)], index
            )
            send[pl.ds(TURN * turn + i, 4, stride=16), :] = found
        first = 4 * FACE_ROWS
        for part, regions in enumerate((LOWER, UPPER)):
            for f, q in enumerate(regions):
                cross_src[4 * part + f : 4 * part + f + 1, :] = source[first + q : first + q + 1, :]
        for part in range(2):
            at = FACE + part * DIAG
            found = pick(
                [cross_src[4 * part : 4 * part + 4, :]], lists_ref[:, at : at + DIAG]
            )
            send[pl.ds(TURN * turn + FACE_ROWS + part, 4, stride=16), :] = found

    def add_received(turn, target):
        def sent_row(i):
            return recv[pl.ds(TURN * turn + i, 4, stride=16), :]

        def diagonal_row(q, i):
            at = 32 * turn + 8 * q + i
            return recv_diag[at : at + 1, :]

        for i in range(FACE_ROWS):
            index = face_inv[pl.ds(i, 4, stride=16), :]
            found = pick([sent_row(j) for j in range(FACE_ROWS)], index)
            target[pl.ds(i, 4, stride=FACE_ROWS), :] += found
        blank = jnp.zeros((2, LANES), jnp.float32)
        lower = sent_row(FACE_ROWS) + jnp.concatenate(
            [blank, diagonal_row(2, 2), diagonal_row(3, 3)], axis=0
        )
        upper = sent_row(FACE_ROWS + 1) + jnp.concatenate(
            [blank, diagonal_row(0, 2), diagonal_row(1, 3)], axis=0
        )
        lower = pick([lower], cross_inv[0:4, :])
        upper = pick([upper], cross_inv[4:8, :])
        first = 4 * FACE_ROWS
        for part, regions in ((lower, LOWER), (upper, UPPER)):
            for f, q in enumerate(regions):
                target[first + q : first + q + 1, :] += part[f : f + 1]

    element = iota((ELEMS, LANES), 0)
    offset = (element * STRIDE) & 127
    is_last = element == live - 1

    def orders(c):
        return order_ref[:, c * LANES : (c + 1) * LANES]

    def last_row(values):
        return jnp.sum(jnp.where(is_last, values, jnp.zeros_like(values)), axis=0, keepdims=True)

    def set_up():
        for f in range(4):
            row = lists_ref[f : f + 1, 0:FACE]
            face_inv[16 * f : 16 * f + 16, :] = inverse_rows(row >> 7, row & 127, 16)
            for part in range(2):
                at = FACE + part * DIAG
                row = lists_ref[f : f + 1, at : at + DIAG]
                number = (iota((8, DIAG), 1) + 1).astype(jnp.float32).astype(jnp.bfloat16)
                found = over_lanes(number, one_hot_lanes(row))
                cross_inv[4 * part + f : 4 * part + f + 1, :] = found[0:1].astype(jnp.int32) - 1
        inv_mult[...] = jnp.ones_like(inv_mult)
        for f in range(4):
            named = face_inv[16 * f : 16 * f + FACE_ROWS, :] >= 0
            inv_mult[f * FACE_ROWS : (f + 1) * FACE_ROWS, :] = jnp.where(named, 0.5, 1.0)
        for q in range(4):
            copies_of = jnp.ones((1, LANES), jnp.float32)
            for part, regions in enumerate((LOWER, UPPER)):
                for f, region in enumerate(regions):
                    if region == q:
                        row = cross_inv[4 * part + f : 4 * part + f + 1, :]
                        copies_of = copies_of + jnp.where(row >= 0, 1.5, 0.0)
            at = 4 * FACE_ROWS + q
            inv_mult[at : at + 1, :] = 1.0 / copies_of

        @pl.loop(0, ELEMS // 8)
        def _(group):
            block = order_ref[pl.ds(pl.multiple_of(8 * group, 8), 8), :]
            for s in range(8):
                e = 8 * group + s
                row = block[s : s + 1]
                shifted = row + lax.rem(e * STRIDE, LANES)
                own = jnp.where(live <= e, 0, jnp.where(live == e + 1, STRIDE, 4 * LANES))
                high = jnp.where(row >= own, 7, shifted >> 7)
                elem_inv[pl.ds(pl.multiple_of(8 * e, 8), 8), :] = inverse_rows(
                    high, shifted & 127, 8
                )

        wrapped = jnp.concatenate([last_row(orders(c)) for c in range(4)], axis=1) - STRIDE
        wrap_inv[...] = inverse_rows(wrapped >> 7, wrapped & 127, 8)

    def derivative(chunks, first):
        swapped = [pltpu.roll(u, 64, 1) for u in chunks]
        result = []
        for out in range(4):
            total = None
            for src in range(4):
                at = first + (out * 4 + src) * 2
                term = coef_ref[at : at + 1, :] * chunks[src]
                total = term if total is None else total + term
                total = total + coef_ref[at + 1 : at + 2, :] * swapped[src]
            result.append(total)
        return result

    def stacked(k):
        return jnp.concatenate(
            [geo_ref[k, :, c * LANES : (c + 1) * LANES] for c in range(4)], axis=0
        )

    def operate(source):
        for e, row in enumerate(ROW_OF):
            windows[8 * e : 8 * e + 8, :] = source[row : row + 8, :]
        rows = [windows[pl.ds(k, ELEMS, stride=8), :] for k in range(5)]
        chunks = []
        for c in range(4):
            order = orders(c)
            around = pick(
                [eight(source[0:1, :]), eight(source[1:2, :])], eight(last_row(order)) - STRIDE
            )[0:1]
            values = pick(rows, order + offset)
            chunks.append(jnp.where(is_last & (order >= STRIDE), around, values))
        exact = lax.Precision.HIGHEST
        narrow = jnp.concatenate(chunks, axis=0)
        grads = jnp.dot(
            narrow, ahead_ref[...], precision=exact, preferred_element_type=jnp.float32
        )
        fluxes = jnp.concatenate(
            [stacked(1) * grads[:, :LANES], stacked(2) * grads[:, LANES:]], axis=1
        )
        terms = jnp.dot(
            fluxes, back_ref[...], precision=exact, preferred_element_type=jnp.float32
        )
        grad = derivative(chunks, 0)
        grad = [geo_ref[0, :, c * LANES : (c + 1) * LANES] * grad[c] for c in range(4)]
        first = derivative(grad, 32)
        factor = shift_ref[...]
        result = [
            terms[c * ELEMS : (c + 1) * ELEMS] + first[c] + factor * chunks[c] for c in range(4)
        ]
        for k in range(5):
            spread[pl.ds(k, ELEMS, stride=8), :] = pick(
                result, elem_inv[pl.ds(k, ELEMS, stride=8), :]
            )
        for e, row in enumerate(ROW_OF):
            sums[e % 3, row : row + 8, :] = spread[8 * e : 8 * e + 8, :]
        sums[0, 0:8, :] += pick([eight(last_row(r)) for r in result], wrap_inv[...])
        return sums[0] + sums[1] + sums[2]

    def dots(*products):
        rows = [jnp.sum(p, axis=0, keepdims=True) for p in products]
        rows.append(jnp.zeros((8 - len(rows), LANES), jnp.float32))
        return jnp.concatenate(rows, axis=0)

    send[...] = jnp.zeros_like(send)
    spread[...] = jnp.zeros_like(spread)
    sums[...] = jnp.zeros_like(sums)
    resid[...] = jnp.zeros_like(resid)
    slot = iota((ROWS, LANES), 0) * LANES + iota((ROWS, LANES), 1)
    resid[0:ROWS, :] = jnp.where(slot < live * STRIDE, rhs_ref[...], 0.0)
    fill_send(0, resid)
    pl.semaphore_wait(barrier, len(everyone))
    exchange = start_exchange(0)
    set_up()
    for copy in exchange:
        copy.wait_recv()
    add_received(0, resid)

    part_w[...] = operate(resid)
    image[...] = part_w[...]
    fill_send(1, image)
    exchange = start_exchange(1)
    res0 = resid[...]
    summing = start_sum(0, 0, dots(res0 * res0 * inv_mult[...], res0 * part_w[...]))
    for copy in exchange:
        copy.wait_recv()
    add_received(1, image)
    summing = start_sum(0, 1, end_sum(0, 0, summing))

    second[...] = operate(image)
    fill_send(2, second)
    exchange = start_exchange(2)
    summing = start_sum(0, 2, end_sum(0, 1, summing))
    totals = jnp.sum(end_sum(0, 2, summing), axis=1, keepdims=True)
    norm0 = totals[0:1]
    energy0 = totals[1:2]
    alpha0 = norm0 / energy0

    res0 = resid[...]
    image0 = image[...]
    res1 = res0 - alpha0 * image0
    scaled = res1 * inv_mult[...]
    block = dots(
        scaled * res1, res1 * (part_w[...] - alpha0 * second[...]), scaled * image0
    )
    summing = start_sum(1, 0, block)
    for copy in exchange:
        copy.wait_recv()
    add_received(2, second)
    summing = start_sum(1, 1, end_sum(1, 0, summing))
    summing = start_sum(1, 2, end_sum(1, 1, summing))
    totals = jnp.sum(end_sum(1, 2, summing), axis=1, keepdims=True)
    norm1 = totals[0:1]
    beta = norm1 / norm0
    energy1 = totals[1:2] + beta * (2.0 * totals[2:3] + beta * energy0)
    alpha1 = norm1 / energy1

    res0 = resid[...]
    image0 = image[...]
    res1 = res0 - alpha0 * image0
    image1 = (image0 - alpha0 * second[...]) + beta * image0
    solved = alpha0 * res0 + alpha1 * (res1 + beta * res0)
    left = res1 - alpha1 * image1
    sol_ref[...] = solved[0:ROWS]
    res_ref[...] = left[0:ROWS]
    for copy in copies:
        copy.wait_send()


def solution(mesh):
    n_px = mesh.shape["px"]
    n_py = mesh.shape["py"]
    low_py = 4 if n_py >= 16 else 2
    count = 3 * 8 + 2 * ((2 * low_py - 1) + (n_px // 2 - 1) + (n_py // low_py - 1))
    coef, ahead, back = tables()

    def body(right_side, geometry, shift, node_order, elem_counts, share_lists):
        vmem = pl.BlockSpec(memory_space=pltpu.VMEM)
        plane = jax.ShapeDtypeStruct((ROWS, LANES), jnp.float32)
        vector = pltpu.VMEM((PAD, LANES), jnp.float32)
        solved, left = pl.pallas_call(
            functools.partial(kernel, n_px, n_py),
            out_shape=(plane, plane),
            in_specs=[vmem] * 9,
            out_specs=(vmem, vmem),
            scratch_shapes=[
                vector,
                vector,
                vector,
                vector,
                pltpu.VMEM((8 * ELEMS + 8, LANES), jnp.float32),
                pltpu.VMEM((8 * ELEMS + 8, LANES), jnp.float32),
                pltpu.VMEM((3, PAD, LANES), jnp.float32),
                pltpu.VMEM((8 * ELEMS + 8, LANES), jnp.int32),
                pltpu.VMEM((80, LANES), jnp.int32),
                pltpu.VMEM((8, LANES), jnp.int32),
                pltpu.VMEM((8, LANES), jnp.int32),
                vector,
                pltpu.VMEM((8, LANES), jnp.float32),
                pltpu.VMEM((3 * TURN, LANES), jnp.float32),
                pltpu.VMEM((3 * TURN, LANES), jnp.float32),
                pltpu.VMEM((3 * 32, LANES), jnp.float32),
                pltpu.VMEM((2, 3, 8, 8, LANES), jnp.float32),
                pltpu.SemaphoreType.DMA((count,)),
                pltpu.SemaphoreType.DMA((count,)),
            ],
            compiler_params=pltpu.CompilerParams(
                collective_id=0, has_side_effects=True, vmem_limit_bytes=32 * 2**20
            ),
            cost_estimate=pl.CostEstimate(
                flops=10**8, bytes_accessed=2 * 10**6, transcendentals=0
            ),
        )(
            right_side.reshape(ROWS, LANES),
            geometry[0, 0],
            shift.reshape(ELEMS, 1),
            node_order[0, 0],
            elem_counts,
            share_lists[0, 0],
            jnp.asarray(coef),
            jnp.asarray(ahead),
            jnp.asarray(back),
        )
        shape = (1, 1, ROWS * LANES)
        return solved.reshape(shape), left.reshape(shape)

    return jax.shard_map(
        body,
        mesh=mesh,
        in_specs=(
            P("px", "py", None),
            P("px", "py", None, None, None),
            P("px", "py", None),
            P("px", "py", None, None),
            P("px", "py"),
            P("px", "py", None, None),
        ),
        out_specs=(P("px", "py", None), P("px", "py", None)),
        check_vma=False,
    )
```

time: 1250 us -> 58.4 us (0.05); the launches traced: 1240 us -> 58.1 us
  other arithmetic: 505 us -> 1.05 us
  local copies, waits for them, and re-layouts: 383 us -> 5.63 us
  blocking collectives: 304 us -> 0 us
  Pallas kernels: 0 us -> 50 us
  starting transfers between devices: 30.9 us -> 0 us
    scatter-add x21 -> x0, other arithmetic: 491 us -> none  [the longest x2 314 us: body(): image = assemble(jnp.zeros((nodes_total,), jnp.float32).at[node_index.res...]
    gather x10 -> x0, local copies, waits for them, and re-layouts: 374 us -> none  [the longest x4 271 us: element_terms(): gathered = jnp.take(values_in, node_index, axis=0)]
    psum x3 -> x0, blocking collectives: 304 us -> none  [the longest x2 205 us: squares(): return lax.psum(jnp.sum(vector * vector * inverse), ('px', 'py'))]
    pallas_call x0 -> x1, Pallas kernels: none -> 50 us  [body(): pl.pallas_call(functools.partial(kernel, n_px, n_py), out_shape=(plane, p...]
    ppermute x12 -> x0, starting transfers between devices: 30.9 us -> none  [the longest x6 16.8 us: padded(): lax.ppermute(tail, axis, [(i, (i + 1) % count) for i in range(ends)])]
  transfers between devices with their start and end apart: 12 -> 0, of which waited for: 2 -> 0; matrix products, arithmetic and copies ran while one was open for 12% -> 0% of each run, Pallas kernels for 0% -> 0%
where the time goes in v1:
time: 58.4 us; the launch traced here: 58.1 us
  Pallas kernels  50 us (86%)
  local copies, waits for them, and re-layouts  5.63 us (10%)
  between operations  1.36 us (2%)
  other arithmetic  1.05 us (2%)
    pallas_call x1, Pallas kernels, body(): pl.pallas_call(functools.partial(kernel, n_px, n_py), out_shape=(plane, p...  50 us
    unnamed x12, local copies, waits for them, and re-layouts  3.5 us
    reshape x2, local copies, waits for them, and re-layouts, body(): return (solved.reshape(shape), left.reshape(shape))  1.39 us

profile of v1, /device:TPU:1, one launch (start us, length us, event | category | flops | bytes accessed | tf_op | source)
XLA Modules:
  0.0 58.1 jit_solution(9163306648407971378)
XLA Ops:
  0.6 0.0 copy-start.1
  1.3 0.7 %copy.11.shift_ref = f32[48,1]{1,0:T(8,128)S(1)} copy(f32[48,1]{0,1:T(1,128)} %bitcast.9) | data formatting | bytes 384 | tf_op jit(solution)/shard_map/reshape | solution.py:516
  2.1 0.0 copy-start.4
  2.1 1.1 %reduce = f32[16512]{0:T(1024)S(1)} reduce(f32[1,1,16512]{2,1,0:T(1,128)} %param.9, f32[]{:T(128)} %constant.15), dimensions={0,1}, to_apply=%param.9.reduce_sub_computation | reduce | bytes 132100 | tf_op args[0]
  3.1 0.0 copy-done.1
  3.1 0.0 copy-done.4
  3.1 0.0 copy-start
  3.2 1.0 %copy-done = f32[1,1,3,48,512]{4,3,2,1,0:T(8,128)S(1)} copy-done((f32[1,1,3,48,512]{4,3,2,1,0:T(8,128)S(1)}, f32[1,1,3,48,512]{4,3,2,1,0:T(8,128)}, u32[]{:S(2)}) %copy-start) | copy-done | bytes 294936
  4.1 0.0 copy-start.2
  4.1 0.9 %copy-done.2 = f32[128,256]{1,0:T(8,128)S(1)} copy-done((f32[128,256]{1,0:T(8,128)S(1)}, f32[128,256]{1,0:T(8,128)}, u32[]{:S(2)}) %copy-start.2) | copy-done | bytes 131096
  5.0 0.0 copy-start.3
  5.0 0.9 %copy-done.3 = s32[1,1,48,512]{3,2,1,0:T(8,128)S(1)} copy-done((s32[1,1,48,512]{3,2,1,0:T(8,128)S(1)}, s32[1,1,48,512]{3,2,1,0:T(8,128)}, u32[]{:S(2)}) %copy-start.3) | copy-done | bytes 98328
  5.9 0.0 copy-start.5
  5.9 0.7 %copy-done.5 = s32[1,1,4,1536]{3,2,1,0:T(4,128)S(1)} copy-done((s32[1,1,4,1536]{3,2,1,0:T(4,128)S(1)}, s32[1,1,4,1536]{3,2,1,0:T(4,128)}, u32[]{:S(2)}) %copy-start.5) | copy-done | bytes 24600
  6.6 50.0 %shard_map.104 = (f32[129,128]{1,0:T(8,128)S(1)}, f32[129,128]{1,0:T(8,128)S(1)}) custom-call(f32[129,128]{1,0:T(8,128)S(1)} %bitcast.6, f32[3,48,512]{2,1,0:T(8,128)S(1)} %bitcast.5, f32[48,1]{1,0:T(8,128)S(1)} %copy.11.shift_ref, s32[48,512]{1,0:T(8,128)S(1)} %bitcast.7, s32[1,1]{1,0:T(1,128)S(6)} %copy.12.count_ref, s32[4,1536]{1,0:T(4,128)S(1)} %bitcast.8, ...), custom_call_target="tpu_custom_call" | custom-call | flops 100000000 | bytes 2000000 | tf_op jit(solution)/shard_map/pallas_call | solution.py:481
  56.7 0.7 %reshape.18 = f32[1,1,16512]{2,1,0:T(1,128)} reshape(f32[129,128]{1,0:T(8,128)S(1)} %get-tuple-element.4) | data formatting | bytes 132096 | tf_op jit(solution)/shard_map/reshape | solution.py:525
  57.4 0.7 %reshape.19 = f32[1,1,16512]{2,1,0:T(1,128)} reshape(f32[129,128]{1,0:T(8,128)S(1)} %get-tuple-element.5) | data formatting | bytes 132096 | tf_op jit(solution)/shard_map/reshape | solution.py:525
Async XLA Ops:
  0.6 2.5 %copy-start.1 = (f32[256,128]{1,0:T(8,128)S(1)}, f32[256,128]{1,0:T(8,128)}, u32[]{:S(2)}) copy-start(f32[256,128]{1,0:T(8,128)} %constant.8.clone.back_ref) | copy-start | bytes 393220
  2.1 1.1 %copy-start.4 = (f32[64,128]{1,0:T(8,128)S(1)}, f32[64,128]{1,0:T(8,128)}, u32[]{:S(2)}) copy-start(f32[64,128]{1,0:T(8,128)} %constant.6.clone.coef_ref) | copy-start | bytes 98308
  3.1 1.0 %copy-start = (f32[1,1,3,48,512]{4,3,2,1,0:T(8,128)S(1)}, f32[1,1,3,48,512]{4,3,2,1,0:T(8,128)}, u32[]{:S(2)}) copy-start(f32[1,1,3,48,512]{4,3,2,1,0:T(8,128)} %param.10) | copy-start | bytes 884740
  4.1 0.9 %copy-start.2 = (f32[128,256]{1,0:T(8,128)S(1)}, f32[128,256]{1,0:T(8,128)}, u32[]{:S(2)}) copy-start(f32[128,256]{1,0:T(8,128)} %constant.7.clone.ahead_ref) | copy-start | bytes 393220
  5.0 0.9 %copy-start.3 = (s32[1,1,48,512]{3,2,1,0:T(8,128)S(1)}, s32[1,1,48,512]{3,2,1,0:T(8,128)}, u32[]{:S(2)}) copy-start(s32[1,1,48,512]{3,2,1,0:T(8,128)} %param.12) | copy-start | bytes 294916
  5.9 0.7 %copy-start.5 = (s32[1,1,4,1536]{3,2,1,0:T(4,128)S(1)}, s32[1,1,4,1536]{3,2,1,0:T(4,128)}, u32[]{:S(2)}) copy-start(s32[1,1,4,1536]{3,2,1,0:T(4,128)} %param.14) | copy-start | bytes 73732

commit v2 on v1

--- a/solution.py
+++ b/solution.py
@@ -118,17 +118,26 @@
 def kernel(
     n_px,
     n_py,
+    rhs_hbm,
+    geo_hbm,
+    shift_hbm,
+    order_hbm,
+    count_ref,
+    lists_hbm,
+    coef_hbm,
+    ahead_hbm,
+    back_hbm,
+    sol_ref,
+    res_ref,
     rhs_ref,
     geo_ref,
     shift_ref,
     order_ref,
-    count_ref,
     lists_ref,
     coef_ref,
     ahead_ref,
     back_ref,
-    sol_ref,
-    res_ref,
+    factors,
     resid,
     image,
     second,
@@ -148,41 +157,42 @@
     red,
     send_sem,
     recv_sem,
+    load_sem,
 ):
+    loads = {}
+    for number, (name, src, dst) in enumerate(
+        (
+            ("lists", lists_hbm, lists_ref),
+            ("rhs", rhs_hbm, rhs_ref),
+            ("order", order_hbm, order_ref),
+            ("shift", shift_hbm, shift_ref),
+            ("ahead", ahead_hbm, ahead_ref),
+            ("geo", geo_hbm, geo_ref),
+            ("back", back_hbm, back_ref),
+            ("coef", coef_hbm, coef_ref),
+        )
+    ):
+        loads[name] = pltpu.make_async_copy(src, dst, load_sem.at[number])
+        loads[name].start()
+
     px = lax.axis_index("px")
     py = lax.axis_index("py")
 
     def moved(step_x, step_y):
         return (lax.rem(px + step_x + n_px, n_px), lax.rem(py + step_y + n_py, n_py))
 
-    low_py = 4 if n_py >= 16 else 2
-    phases = (
-        ((1, 2), (1, low_py)),
-        ((2, n_px // 2), (1, 1)),
-        ((1, 1), (low_py, n_py // low_py)),
-    )
-
-    def place(phase):
-        (stride_x, size_x), (stride_y, size_y) = phase
-        at_x = lax.rem(px // stride_x, size_x)
-        at_y = lax.rem(py // stride_y, size_y)
-        return at_x, at_y
-
-    def partners(phase):
-        (stride_x, size_x), (stride_y, size_y) = phase
-        at_x, at_y = place(phase)
-        found = []
-        for dx in range(size_x):
-            for dy in range(size_y):
-                if dx or dy:
-                    to_x = lax.rem(at_x + dx, size_x)
-                    to_y = lax.rem(at_y + dy, size_y)
-                    found.append((px + (to_x - at_x) * stride_x, py + (to_y - at_y) * stride_y))
-        return found
+    sizes = (n_px, n_py)
+
+    def place(stage):
+        return px if stage == 0 else py
+
+    def partners(stage):
+        if stage == 0:
+            return [(lax.rem(px + d, n_px), py) for d in range(1, n_px)]
+        return [(px, lax.rem(py + d, n_py)) for d in range(1, n_py)]
 
     everyone = [moved(*step) for step in FACE_STEPS + DIAG_STEPS]
-    for phase in phases:
-        everyone += partners(phase)
+    everyone += partners(0) + partners(1)
     barrier = pltpu.get_barrier_semaphore()
     for other in everyone:
         pl.semaphore_signal(
@@ -225,24 +235,20 @@
             )
         return started
 
-    def start_sum(turn, number, block):
-        phase = phases[number]
-        at_x, at_y = place(phase)
-        mine = at_x * phase[1][1] + at_y
-        red[turn, number, pl.ds(mine, 1)] = block[None]
-        return [
-            start_copy(red.at[turn, number, mine], red.at[turn, number, mine], other)
-            for other in partners(phase)
-        ]
-
-    def end_sum(turn, number, started):
+    def start_sum(turn, stage, row):
+        first = turn * (n_px + n_py) + stage * n_px
+        mine = first + place(stage)
+        red[pl.ds(mine, 1)] = row[None]
+        return [start_copy(red.at[mine], red.at[mine], other) for other in partners(stage)]
+
+    def end_sum(turn, stage, started):
+        first = turn * (n_px + n_py) + stage * n_px
         for copy in started:
             copy.wait_recv()
-        size = phases[number][0][1] * phases[number][1][1]
-        total = red[turn, number, 0]
-        for slot in range(1, size):
-            total = total + red[turn, number, slot]
-        return total
+        sums_of = [red[first + slot] for slot in range(sizes[stage])]
+        while len(sums_of) > 1:
+            sums_of = [x + y for x, y in zip(sums_of[::2], sums_of[1::2])]
+        return sums_of[0]
 
     live = count_ref[...]
 
@@ -384,7 +390,7 @@
         grad = derivative(chunks, 0)
         grad = [geo_ref[0, :, c * LANES : (c + 1) * LANES] * grad[c] for c in range(4)]
         first = derivative(grad, 32)
-        factor = shift_ref[...]
+        factor = factors[...]
         result = [
             terms[c * ELEMS : (c + 1) * ELEMS] + first[c] + factor * chunks[c] for c in range(4)
         ]
@@ -398,61 +404,74 @@
         return sums[0] + sums[1] + sums[2]
 
     def dots(*products):
-        rows = [jnp.sum(p, axis=0, keepdims=True) for p in products]
-        rows.append(jnp.zeros((8 - len(rows), LANES), jnp.float32))
-        return jnp.concatenate(rows, axis=0)
+        lane = iota((1, LANES), 1)
+        row = jnp.zeros((1, LANES), jnp.float32)
+        for k, product in enumerate(products):
+            total = jnp.sum(jnp.sum(product, axis=0, keepdims=True), axis=1, keepdims=True)
+            row = jnp.where(lane == k, total, row)
+        return row
 
     send[...] = jnp.zeros_like(send)
     spread[...] = jnp.zeros_like(spread)
     sums[...] = jnp.zeros_like(sums)
     resid[...] = jnp.zeros_like(resid)
+    loads["lists"].wait()
+    loads["rhs"].wait()
+    for i in range(ROWS):
+        resid[i : i + 1, :] = rhs_ref[:, i * LANES : (i + 1) * LANES]
     slot = iota((ROWS, LANES), 0) * LANES + iota((ROWS, LANES), 1)
-    resid[0:ROWS, :] = jnp.where(slot < live * STRIDE, rhs_ref[...], 0.0)
+    resid[0:ROWS, :] = jnp.where(slot < live * STRIDE, resid[0:ROWS, :], 0.0)
     fill_send(0, resid)
     pl.semaphore_wait(barrier, len(everyone))
     exchange = start_exchange(0)
+    loads["order"].wait()
+    loads["shift"].wait()
     set_up()
+    same = iota((ELEMS, ELEMS), 0) == iota((ELEMS, ELEMS), 1)
+    column = jnp.sum(jnp.where(same, shift_ref[...], 0.0), axis=1, keepdims=True)
+    factors[...] = jnp.broadcast_to(column, (ELEMS, LANES))
+    for name in ("ahead", "geo", "back", "coef"):
+        loads[name].wait()
     for copy in exchange:
         copy.wait_recv()
     add_received(0, resid)
 
     part_w[...] = operate(resid)
+    res0 = resid[...]
+    summing = start_sum(0, 0, dots(res0 * res0 * inv_mult[...], res0 * part_w[...]))
     image[...] = part_w[...]
     fill_send(1, image)
     exchange = start_exchange(1)
-    res0 = resid[...]
-    summing = start_sum(0, 0, dots(res0 * res0 * inv_mult[...], res0 * part_w[...]))
+    summing = start_sum(0, 1, end_sum(0, 0, summing))
     for copy in exchange:
         copy.wait_recv()
     add_received(1, image)
-    summing = start_sum(0, 1, end_sum(0, 0, summing))
 
     second[...] = operate(image)
     fill_send(2, second)
     exchange = start_exchange(2)
-    summing = start_sum(0, 2, end_sum(0, 1, summing))
-    totals = jnp.sum(end_sum(0, 2, summing), axis=1, keepdims=True)
-    norm0 = totals[0:1]
-    energy0 = totals[1:2]
+    totals = end_sum(0, 1, summing)
+    norm0 = totals[:, 0:1]
+    energy0 = totals[:, 1:2]
     alpha0 = norm0 / energy0
 
     res0 = resid[...]
     image0 = image[...]
     res1 = res0 - alpha0 * image0
     scaled = res1 * inv_mult[...]
-    block = dots(
-        scaled * res1, res1 * (part_w[...] - alpha0 * second[...]), scaled * image0
-    )
-    summing = start_sum(1, 0, block)
+    row = dots(scaled * res1, res1 * (part_w[...] - alpha0 * second[...]), scaled * image0)
+    summing = start_sum(1, 0, row)
     for copy in exchange:
         copy.wait_recv()
     add_received(2, second)
+    earlier = list(copies)
     summing = start_sum(1, 1, end_sum(1, 0, summing))
-    summing = start_sum(1, 2, end_sum(1, 1, summing))
-    totals = jnp.sum(end_sum(1, 2, summing), axis=1, keepdims=True)
-    norm1 = totals[0:1]
+    for copy in earlier:
+        copy.wait_send()
+    totals = end_sum(1, 1, summing)
+    norm1 = totals[:, 0:1]
     beta = norm1 / norm0
-    energy1 = totals[1:2] + beta * (2.0 * totals[2:3] + beta * energy0)
+    energy1 = totals[:, 1:2] + beta * (2.0 * totals[:, 2:3] + beta * energy0)
     alpha1 = norm1 / energy1
 
     res0 = resid[...]
@@ -463,27 +482,36 @@
     left = res1 - alpha1 * image1
     sol_ref[...] = solved[0:ROWS]
     res_ref[...] = left[0:ROWS]
-    for copy in copies:
+    for copy in summing:
         copy.wait_send()
 
 
 def solution(mesh):
     n_px = mesh.shape["px"]
     n_py = mesh.shape["py"]
-    low_py = 4 if n_py >= 16 else 2
-    count = 3 * 8 + 2 * ((2 * low_py - 1) + (n_px // 2 - 1) + (n_py // low_py - 1))
+    count = 3 * 8 + 2 * (n_px - 1 + n_py - 1)
     coef, ahead, back = tables()
 
     def body(right_side, geometry, shift, node_order, elem_counts, share_lists):
         vmem = pl.BlockSpec(memory_space=pltpu.VMEM)
+        hbm = pl.BlockSpec(memory_space=pltpu.HBM)
         plane = jax.ShapeDtypeStruct((ROWS, LANES), jnp.float32)
         vector = pltpu.VMEM((PAD, LANES), jnp.float32)
         solved, left = pl.pallas_call(
             functools.partial(kernel, n_px, n_py),
             out_shape=(plane, plane),
-            in_specs=[vmem] * 9,
+            in_specs=[hbm] * 4 + [vmem] + [hbm] * 4,
             out_specs=(vmem, vmem),
             scratch_shapes=[
+                pltpu.VMEM((1, ROWS * LANES), jnp.float32),
+                pltpu.VMEM((3, ELEMS, 4 * LANES), jnp.float32),
+                pltpu.VMEM((1, ELEMS), jnp.float32),
+                pltpu.VMEM((ELEMS, 4 * LANES), jnp.int32),
+                pltpu.VMEM((4, FACE + 2 * DIAG), jnp.int32),
+                pltpu.VMEM(coef.shape, jnp.float32),
+                pltpu.VMEM(ahead.shape, jnp.float32),
+                pltpu.VMEM(back.shape, jnp.float32),
+                pltpu.VMEM((ELEMS, LANES), jnp.float32),
                 vector,
                 vector,
                 vector,
@@ -500,20 +528,21 @@
                 pltpu.VMEM((3 * TURN, LANES), jnp.float32),
                 pltpu.VMEM((3 * TURN, LANES), jnp.float32),
                 pltpu.VMEM((3 * 32, LANES), jnp.float32),
-                pltpu.VMEM((2, 3, 8, 8, LANES), jnp.float32),
+                pltpu.VMEM((2 * (n_px + n_py), 1, LANES), jnp.float32),
                 pltpu.SemaphoreType.DMA((count,)),
                 pltpu.SemaphoreType.DMA((count,)),
+                pltpu.SemaphoreType.DMA((8,)),
             ],
             compiler_params=pltpu.CompilerParams(
-                collective_id=0, has_side_effects=True, vmem_limit_bytes=32 * 2**20
+                collective_id=0, has_side_effects=True, vmem_limit_bytes=60 * 2**20
             ),
             cost_estimate=pl.CostEstimate(
                 flops=10**8, bytes_accessed=2 * 10**6, transcendentals=0
             ),
         )(
-            right_side.reshape(ROWS, LANES),
+            right_side[0],
             geometry[0, 0],
-            shift.reshape(ELEMS, 1),
+            shift[0],
             node_order[0, 0],
             elem_counts,
             share_lists[0, 0],

time: 58.4 us -> 49.5 us (0.85)
  Pallas kernels: 50 us -> 45.7 us
  local copies, waits for them, and re-layouts: 5.63 us -> 2.31 us
  other arithmetic: 1.05 us -> 0 us
    pallas_call x1, Pallas kernels: 50 us -> 45.7 us  [body(): pl.pallas_call(functools.partial(kernel, n_px, n_py), out_shape=(plane, p...]
    unnamed x12 -> x2, local copies, waits for them, and re-layouts: 3.5 us -> 0.01 us
    unnamed x1 -> x0, other arithmetic: 1.05 us -> none
    reshape x2, local copies, waits for them, and re-layouts: 1.39 us -> 2.3 us  [body(): return (solved.reshape(shape), left.reshape(shape))]
    reshape x1 -> x0, local copies, waits for them, and re-layouts: 0.74 us -> none  [body(): shift.reshape(ELEMS, 1)]
where the time goes in v2:
time: 49.5 us; the launch traced here: 49.3 us
  Pallas kernels  45.7 us (92%)
  local copies, waits for them, and re-layouts  2.31 us (5%)
  between operations  1.29 us (3%)
    pallas_call x1, Pallas kernels, body(): pl.pallas_call(functools.partial(kernel, n_px, n_py), out_shape=(plane, p...  45.7 us
    reshape x2, local copies, waits for them, and re-layouts, body(): return (solved.reshape(shape), left.reshape(shape))  2.3 us

profile of v2, /device:TPU:1, one launch (start us, length us, event | category | flops | bytes accessed | tf_op | source)
XLA Modules:
  0.0 49.3 jit_solution(7080487867698830089)
XLA Ops:
  1.3 45.7 %shard_map.104 = (f32[129,128]{1,0:T(8,128)}, f32[129,128]{1,0:T(8,128)}) custom-call(f32[1,16512]{1,0:T(1,128)} %bitcast.7, f32[3,48,512]{2,1,0:T(8,128)} %bitcast.5, f32[1,48]{1,0:T(1,128)} %bitcast.9, s32[48,512]{1,0:T(8,128)} %bitcast.6, s32[1,1]{1,0:T(1,128)S(6)} %copy.11.count_ref, s32[4,1536]{1,0:T(4,128)} %bitcast.8, ...), custom_call_target="tpu_custom_call" | custom-call | flops 100000000 | bytes 2000000 | tf_op jit(solution)/shard_map/pallas_call | solution.py:500
  47.0 0.0 copy-start
  47.0 1.6 %reshape.10 = f32[1,1,16512]{2,1,0:T(1,128)} reshape(f32[129,128]{1,0:T(8,128)} %get-tuple-element.4) | data formatting | bytes 132096 | tf_op jit(solution)/shard_map/reshape | solution.py:554
  48.6 0.0 copy-done
  48.6 0.7 %reshape.11 = f32[1,1,16512]{2,1,0:T(1,128)} reshape(f32[129,128]{1,0:T(8,128)S(1)} %copy-done) | data formatting | bytes 132096 | tf_op jit(solution)/shard_map/reshape | solution.py:554
Async XLA Ops:
  47.0 1.6 %copy-start = (f32[129,128]{1,0:T(8,128)S(1)}, f32[129,128]{1,0:T(8,128)}, u32[]{:S(2)}) copy-start(f32[129,128]{1,0:T(8,128)} %get-tuple-element.5) | copy-start | bytes 198148

commit v3 on v2

--- a/solution.py
+++ b/solution.py
@@ -81,8 +81,8 @@
     lanes = index & 127
     total = None
     for j, source in enumerate(sources):
-        term = jnp.where(high == j, take_lanes(source, lanes), 0.0)
-        total = term if total is None else total + term
+        found = take_lanes(source, lanes)
+        total = jnp.where(high == j, found, 0.0 if total is None else total)
     return total
 
 
@@ -151,6 +151,10 @@
     wrap_inv,
     inv_mult,
     cross_src,
+    stack,
+    list_idx,
+    inv_idx,
+    wrap_idx,
     send,
     recv,
     recv_diag,
@@ -252,49 +256,47 @@
 
     live = count_ref[...]
 
+    half = FACE_ROWS // 2
+
+    def pair_up(target, at, upper, lower):
+        target[at : at + 4, :] = upper
+        target[at + 4 : at + 8, :] = lower
+
+    def stack_rows(source, first, step):
+        for j in range(FACE_ROWS):
+            rows = source[pl.ds(first + j, 4, stride=step), :]
+            pair_up(stack, 8 * j, rows, rows)
+        return [stack[8 * j : 8 * j + 8, :] for j in range(FACE_ROWS)]
+
     def fill_send(turn, source):
-        for i in range(FACE_ROWS):
-            index = lists_ref[:, i * LANES : (i + 1) * LANES]
-            found = pick(
-                [source[pl.ds(j, 4, stride=FACE_ROWS), :] for j in range(FACE_ROWS)], index
-            )
-            send[pl.ds(TURN * turn + i, 4, stride=16), :] = found
+        rows = stack_rows(source, 0, FACE_ROWS)
+        for i in range(half):
+            found = pick(rows, list_idx[8 * i : 8 * i + 8, :])
+            send[pl.ds(TURN * turn + i, 4, stride=16), :] = found[0:4]
+            send[pl.ds(TURN * turn + i + half, 4, stride=16), :] = found[4:8]
         first = 4 * FACE_ROWS
-        for part, regions in enumerate((LOWER, UPPER)):
-            for f, q in enumerate(regions):
-                cross_src[4 * part + f : 4 * part + f + 1, :] = source[first + q : first + q + 1, :]
+        for at, q in enumerate(LOWER + UPPER):
+            cross_src[at : at + 1, :] = source[first + q : first + q + 1, :]
+        found = pick([cross_src[...]], list_idx[8 * half : 8 * half + 8, :])
+        send[pl.ds(TURN * turn + FACE_ROWS, 4, stride=16), :] = found[0:4]
+        send[pl.ds(TURN * turn + FACE_ROWS + 1, 4, stride=16), :] = found[4:8]
+
+    def add_received(turn, target):
+        rows = stack_rows(recv, TURN * turn, 16)
+        for i in range(half):
+            found = pick(rows, inv_idx[8 * i : 8 * i + 8, :])
+            target[pl.ds(i, 4, stride=FACE_ROWS), :] += found[0:4]
+            target[pl.ds(i + half, 4, stride=FACE_ROWS), :] += found[4:8]
         for part in range(2):
-            at = FACE + part * DIAG
-            found = pick(
-                [cross_src[4 * part : 4 * part + 4, :]], lists_ref[:, at : at + DIAG]
-            )
-            send[pl.ds(TURN * turn + FACE_ROWS + part, 4, stride=16), :] = found
-
-    def add_received(turn, target):
-        def sent_row(i):
-            return recv[pl.ds(TURN * turn + i, 4, stride=16), :]
-
-        def diagonal_row(q, i):
+            at = TURN * turn + FACE_ROWS + part
+            cross_src[4 * part : 4 * part + 4, :] = recv[pl.ds(at, 4, stride=16), :]
+        for row, q, i in ((2, 2, 2), (3, 3, 3), (6, 0, 2), (7, 1, 3)):
             at = 32 * turn + 8 * q + i
-            return recv_diag[at : at + 1, :]
-
-        for i in range(FACE_ROWS):
-            index = face_inv[pl.ds(i, 4, stride=16), :]
-            found = pick([sent_row(j) for j in range(FACE_ROWS)], index)
-            target[pl.ds(i, 4, stride=FACE_ROWS), :] += found
-        blank = jnp.zeros((2, LANES), jnp.float32)
-        lower = sent_row(FACE_ROWS) + jnp.concatenate(
-            [blank, diagonal_row(2, 2), diagonal_row(3, 3)], axis=0
-        )
-        upper = sent_row(FACE_ROWS + 1) + jnp.concatenate(
-            [blank, diagonal_row(0, 2), diagonal_row(1, 3)], axis=0
-        )
-        lower = pick([lower], cross_inv[0:4, :])
-        upper = pick([upper], cross_inv[4:8, :])
+            cross_src[row : row + 1, :] += recv_diag[at : at + 1, :]
+        found = pick([cross_src[...]], cross_inv[...])
         first = 4 * FACE_ROWS
-        for part, regions in ((lower, LOWER), (upper, UPPER)):
-            for f, q in enumerate(regions):
-                target[first + q : first + q + 1, :] += part[f : f + 1]
+        for at, q in enumerate(LOWER + UPPER):
+            target[first + q : first + q + 1, :] += found[at : at + 1]
 
     element = iota((ELEMS, LANES), 0)
     offset = (element * STRIDE) & 127
@@ -316,6 +318,13 @@
                 number = (iota((8, DIAG), 1) + 1).astype(jnp.float32).astype(jnp.bfloat16)
                 found = over_lanes(number, one_hot_lanes(row))
                 cross_inv[4 * part + f : 4 * part + f + 1, :] = found[0:1].astype(jnp.int32) - 1
+        for i in range(half):
+            pair_up(
+                inv_idx,
+                8 * i,
+                face_inv[pl.ds(i, 4, stride=16), :],
+                face_inv[pl.ds(i + half, 4, stride=16), :],
+            )
         inv_mult[...] = jnp.ones_like(inv_mult)
         for f in range(4):
             named = face_inv[16 * f : 16 * f + FACE_ROWS, :] >= 0
@@ -345,6 +354,7 @@
 
         wrapped = jnp.concatenate([last_row(orders(c)) for c in range(4)], axis=1) - STRIDE
         wrap_inv[...] = inverse_rows(wrapped >> 7, wrapped & 127, 8)
+        wrap_idx[...] = eight(wrapped)
 
     def derivative(chunks, first):
         swapped = [pltpu.roll(u, 64, 1) for u in chunks]
@@ -372,7 +382,8 @@
         for c in range(4):
             order = orders(c)
             around = pick(
-                [eight(source[0:1, :]), eight(source[1:2, :])], eight(last_row(order)) - STRIDE
+                [eight(source[0:1, :]), eight(source[1:2, :])],
+                wrap_idx[:, c * LANES : (c + 1) * LANES],
             )[0:1]
             values = pick(rows, order + offset)
             chunks.append(jnp.where(is_last & (order >= STRIDE), around, values))
@@ -417,6 +428,19 @@
     resid[...] = jnp.zeros_like(resid)
     loads["lists"].wait()
     loads["rhs"].wait()
+    for i in range(half):
+        pair_up(
+            list_idx,
+            8 * i,
+            lists_ref[:, i * LANES : (i + 1) * LANES],
+            lists_ref[:, (i + half) * LANES : (i + half + 1) * LANES],
+        )
+    pair_up(
+        list_idx,
+        8 * half,
+        lists_ref[:, FACE : FACE + DIAG],
+        lists_ref[:, FACE + DIAG : FACE + 2 * DIAG],
+    )
     for i in range(ROWS):
         resid[i : i + 1, :] = rhs_ref[:, i * LANES : (i + 1) * LANES]
     slot = iota((ROWS, LANES), 0) * LANES + iota((ROWS, LANES), 1)
@@ -496,6 +520,10 @@
         vmem = pl.BlockSpec(memory_space=pltpu.VMEM)
         hbm = pl.BlockSpec(memory_space=pltpu.HBM)
         plane = jax.ShapeDtypeStruct((ROWS, LANES), jnp.float32)
+
+        def stay(x):
+            return pltpu.with_memory_space_constraint(x, pltpu.HBM)
+
         vector = pltpu.VMEM((PAD, LANES), jnp.float32)
         solved, left = pl.pallas_call(
             functools.partial(kernel, n_px, n_py),
@@ -525,6 +553,10 @@
                 pltpu.VMEM((8, LANES), jnp.int32),
                 vector,
                 pltpu.VMEM((8, LANES), jnp.float32),
+                pltpu.VMEM((8 * FACE_ROWS, LANES), jnp.float32),
+                pltpu.VMEM((4 * FACE_ROWS + 8, LANES), jnp.int32),
+                pltpu.VMEM((4 * FACE_ROWS, LANES), jnp.int32),
+                pltpu.VMEM((8, 4 * LANES), jnp.int32),
                 pltpu.VMEM((3 * TURN, LANES), jnp.float32),
                 pltpu.VMEM((3 * TURN, LANES), jnp.float32),
                 pltpu.VMEM((3 * 32, LANES), jnp.float32),
@@ -534,21 +566,21 @@
                 pltpu.SemaphoreType.DMA((8,)),
             ],
             compiler_params=pltpu.CompilerParams(
-                collective_id=0, has_side_effects=True, vmem_limit_bytes=60 * 2**20
+                collective_id=0, has_side_effects=True, vmem_limit_bytes=32 * 2**20
             ),
             cost_estimate=pl.CostEstimate(
                 flops=10**8, bytes_accessed=2 * 10**6, transcendentals=0
             ),
         )(
-            right_side[0],
-            geometry[0, 0],
-            shift[0],
-            node_order[0, 0],
+            stay(right_side[0]),
+            stay(geometry[0, 0]),
+            stay(shift[0]),
+            stay(node_order[0, 0]),
             elem_counts,
-            share_lists[0, 0],
-            jnp.asarray(coef),
-            jnp.asarray(ahead),
-            jnp.asarray(back),
+            stay(share_lists[0, 0]),
+            stay(jnp.asarray(coef)),
+            stay(jnp.asarray(ahead)),
+            stay(jnp.asarray(back)),
         )
         shape = (1, 1, ROWS * LANES)
         return solved.reshape(shape), left.reshape(shape)

time: 49.5 us -> 47.7 us (0.964)
  local copies, waits for them, and re-layouts: 2.31 us -> 1.39 us
  Pallas kernels: 45.7 us -> 44.8 us
    reshape x2, local copies, waits for them, and re-layouts: 2.3 us -> 1.39 us  [body(): return (solved.reshape(shape), left.reshape(shape))]
    pallas_call x1, Pallas kernels: 45.7 us -> 44.8 us  [body(): pl.pallas_call(functools.partial(kernel, n_px, n_py), out_shape=(plane, p...]
where the time goes in v3:
time: 47.7 us; the launch traced here: 47.5 us
  Pallas kernels  44.8 us (94%)
  local copies, waits for them, and re-layouts  1.39 us (3%)
  between operations  1.29 us (3%)
    pallas_call x1, Pallas kernels, body(): pl.pallas_call(functools.partial(kernel, n_px, n_py), out_shape=(plane, p...  44.8 us
    reshape x2, local copies, waits for them, and re-layouts, body(): return (solved.reshape(shape), left.reshape(shape))  1.39 us

profile of v3, /device:TPU:1, one launch (start us, length us, event | category | flops | bytes accessed | tf_op | source)
XLA Modules:
  0.0 47.5 jit_solution(1219702383561344596)
XLA Ops:
  1.3 44.8 %shard_map.104 = (f32[129,128]{1,0:T(8,128)S(1)}, f32[129,128]{1,0:T(8,128)S(1)}) custom-call(f32[1,16512]{1,0:T(1,128)} %bitcast.7, f32[3,48,512]{2,1,0:T(8,128)} %bitcast.5, f32[1,48]{1,0:T(1,128)} %bitcast.9, s32[48,512]{1,0:T(8,128)} %bitcast.6, s32[1,1]{1,0:T(1,128)S(6)} %copy.11.count_ref, s32[4,1536]{1,0:T(4,128)} %bitcast.8, ...), custom_call_target="tpu_custom_call" | custom-call | flops 100000000 | bytes 2000000 | tf_op jit(solution)/shard_map/pallas_call | solution.py:528
  46.1 0.7 %reshape.10 = f32[1,1,16512]{2,1,0:T(1,128)} reshape(f32[129,128]{1,0:T(8,128)S(1)} %get-tuple-element.4) | data formatting | bytes 132096 | tf_op jit(solution)/shard_map/reshape | solution.py:586
  46.8 0.7 %reshape.11 = f32[1,1,16512]{2,1,0:T(1,128)} reshape(f32[129,128]{1,0:T(8,128)S(1)} %get-tuple-element.5) | data formatting | bytes 132096 | tf_op jit(solution)/shard_map/reshape | solution.py:586

commit v4 on v3

--- a/solution.py
+++ b/solution.py
@@ -138,10 +138,8 @@
     ahead_ref,
     back_ref,
     factors,
-    resid,
-    image,
-    second,
-    part_w,
+    vec,
+    parts,
     windows,
     spread,
     sums,
@@ -190,24 +188,30 @@
     def place(stage):
         return px if stage == 0 else py
 
-    def partners(stage):
+    def partner(stage, d):
         if stage == 0:
-            return [(lax.rem(px + d, n_px), py) for d in range(1, n_px)]
-        return [(px, lax.rem(py + d, n_py)) for d in range(1, n_py)]
-
-    everyone = [moved(*step) for step in FACE_STEPS + DIAG_STEPS]
-    everyone += partners(0) + partners(1)
+            return (lax.rem(px + d, n_px), py)
+        return (px, lax.rem(py + d, n_py))
+
+    def each_partner(stage, act):
+        @pl.loop(1, sizes[stage])
+        def _(d):
+            act(d)
+
     barrier = pltpu.get_barrier_semaphore()
-    for other in everyone:
+
+    def greet(other):
         pl.semaphore_signal(
             barrier, inc=1, device_id=other, device_id_type=pl.DeviceIdType.MESH
         )
 
-    copies = []
-
-    def start_copy(src, dst, other):
-        number = len(copies)
-        copy = pltpu.make_async_remote_copy(
+    for step in FACE_STEPS + DIAG_STEPS:
+        greet(moved(*step))
+    for stage in range(2):
+        each_partner(stage, lambda d, stage=stage: greet(partner(stage, d)))
+
+    def remote(src, dst, number, other):
+        return pltpu.make_async_remote_copy(
             src_ref=src,
             dst_ref=dst,
             send_sem=send_sem.at[number],
@@ -215,44 +219,49 @@
             device_id=other,
             device_id_type=pl.DeviceIdType.MESH,
         )
-        copy.start()
-        copies.append(copy)
-        return copy
-
-    def start_exchange(turn):
-        started = []
+
+    def exchange(turn):
+        copies = []
         for f, step in enumerate(FACE_STEPS):
-            started.append(
-                start_copy(
-                    send.at[pl.ds(TURN * turn + 16 * f, 16)],
-                    recv.at[pl.ds(TURN * turn + 16 * (f ^ 1), 16)],
+            copies.append(
+                remote(
+                    send.at[turn, pl.ds(16 * f, 16)],
+                    recv.at[turn, pl.ds(16 * (f ^ 1), 16)],
+                    8 * turn + f,
                     moved(*step),
                 )
             )
         for d, step in enumerate(DIAG_STEPS):
-            started.append(
-                start_copy(
-                    send.at[pl.ds(TURN * turn + 16 * DIAG_LIST[d] + 8, 8)],
-                    recv_diag.at[pl.ds(32 * turn + 8 * (3 - d), 8)],
+            copies.append(
+                remote(
+                    send.at[turn, pl.ds(16 * DIAG_LIST[d] + 8, 8)],
+                    recv_diag.at[turn, pl.ds(8 * (3 - d), 8)],
+                    8 * turn + 4 + d,
                     moved(*step),
                 )
             )
-        return started
+        return copies
+
+    def sum_copy(turn, stage, d):
+        mine = turn * (n_px + n_py) + stage * n_px + place(stage)
+        number = 24 + turn * (n_px + n_py - 2) + stage * (n_px - 1) + d - 1
+        return remote(red.at[mine], red.at[mine], number, partner(stage, d))
 
     def start_sum(turn, stage, row):
+        mine = turn * (n_px + n_py) + stage * n_px + place(stage)
+        red[pl.ds(mine, 1)] = row[None]
+        each_partner(stage, lambda d: sum_copy(turn, stage, d).start())
+
+    def end_sum(turn, stage):
+        each_partner(stage, lambda d: sum_copy(turn, stage, d).wait_recv())
         first = turn * (n_px + n_py) + stage * n_px
-        mine = first + place(stage)
-        red[pl.ds(mine, 1)] = row[None]
-        return [start_copy(red.at[mine], red.at[mine], other) for other in partners(stage)]
-
-    def end_sum(turn, stage, started):
-        first = turn * (n_px + n_py) + stage * n_px
-        for copy in started:
-            copy.wait_recv()
-        sums_of = [red[first + slot] for slot in range(sizes[stage])]
-        while len(sums_of) > 1:
-            sums_of = [x + y for x, y in zip(sums_of[::2], sums_of[1::2])]
-        return sums_of[0]
+        rows = [red[first + slot] for slot in range(sizes[stage])]
+        while len(rows) > 1:
+            rows = [x + y for x, y in zip(rows[::2], rows[1::2])]
+        return rows[0]
+
+    def sum_left(turn, stage):
+        each_partner(stage, lambda d: sum_copy(turn, stage, d).wait_send())
 
     live = count_ref[...]
 
@@ -262,37 +271,37 @@
         target[at : at + 4, :] = upper
         target[at + 4 : at + 8, :] = lower
 
-    def stack_rows(source, first, step):
+    def stack_rows(source, step):
         for j in range(FACE_ROWS):
-            rows = source[pl.ds(first + j, 4, stride=step), :]
+            rows = source[pl.ds(j, 4, stride=step), :]
             pair_up(stack, 8 * j, rows, rows)
         return [stack[8 * j : 8 * j + 8, :] for j in range(FACE_ROWS)]
 
     def fill_send(turn, source):
-        rows = stack_rows(source, 0, FACE_ROWS)
+        rows = stack_rows(source, FACE_ROWS)
         for i in range(half):
             found = pick(rows, list_idx[8 * i : 8 * i + 8, :])
-            send[pl.ds(TURN * turn + i, 4, stride=16), :] = found[0:4]
-            send[pl.ds(TURN * turn + i + half, 4, stride=16), :] = found[4:8]
+            send[turn, pl.ds(i, 4, stride=16), :] = found[0:4]
+            send[turn, pl.ds(i + half, 4, stride=16), :] = found[4:8]
         first = 4 * FACE_ROWS
         for at, q in enumerate(LOWER + UPPER):
             cross_src[at : at + 1, :] = source[first + q : first + q + 1, :]
         found = pick([cross_src[...]], list_idx[8 * half : 8 * half + 8, :])
-        send[pl.ds(TURN * turn + FACE_ROWS, 4, stride=16), :] = found[0:4]
-        send[pl.ds(TURN * turn + FACE_ROWS + 1, 4, stride=16), :] = found[4:8]
+        send[turn, pl.ds(FACE_ROWS, 4, stride=16), :] = found[0:4]
+        send[turn, pl.ds(FACE_ROWS + 1, 4, stride=16), :] = found[4:8]
 
     def add_received(turn, target):
-        rows = stack_rows(recv, TURN * turn, 16)
+        rows = stack_rows(recv.at[turn], 16)
         for i in range(half):
             found = pick(rows, inv_idx[8 * i : 8 * i + 8, :])
             target[pl.ds(i, 4, stride=FACE_ROWS), :] += found[0:4]
             target[pl.ds(i + half, 4, stride=FACE_ROWS), :] += found[4:8]
         for part in range(2):
-            at = TURN * turn + FACE_ROWS + part
-            cross_src[4 * part : 4 * part + 4, :] = recv[pl.ds(at, 4, stride=16), :]
+            rows = recv[turn, pl.ds(FACE_ROWS + part, 4, stride=16), :]
+            cross_src[4 * part : 4 * part + 4, :] = rows
         for row, q, i in ((2, 2, 2), (3, 3, 3), (6, 0, 2), (7, 1, 3)):
-            at = 32 * turn + 8 * q + i
-            cross_src[row : row + 1, :] += recv_diag[at : at + 1, :]
+            at = 8 * q + i
+            cross_src[row : row + 1, :] += recv_diag[turn, at : at + 1, :]
         found = pick([cross_src[...]], cross_inv[...])
         first = 4 * FACE_ROWS
         for at, q in enumerate(LOWER + UPPER):
@@ -425,7 +434,8 @@
     send[...] = jnp.zeros_like(send)
     spread[...] = jnp.zeros_like(spread)
     sums[...] = jnp.zeros_like(sums)
-    resid[...] = jnp.zeros_like(resid)
+    resid, image, second = (vec.at[k] for k in range(3))
+    resid[...] = jnp.zeros((PAD, LANES), jnp.float32)
     loads["lists"].wait()
     loads["rhs"].wait()
     for i in range(half):
@@ -446,8 +456,9 @@
     slot = iota((ROWS, LANES), 0) * LANES + iota((ROWS, LANES), 1)
     resid[0:ROWS, :] = jnp.where(slot < live * STRIDE, resid[0:ROWS, :], 0.0)
     fill_send(0, resid)
-    pl.semaphore_wait(barrier, len(everyone))
-    exchange = start_exchange(0)
+    pl.semaphore_wait(barrier, 8 + (n_px - 1) + (n_py - 1))
+    for copy in exchange(0):
+        copy.start()
     loads["order"].wait()
     loads["shift"].wait()
     set_up()
@@ -456,25 +467,30 @@
     factors[...] = jnp.broadcast_to(column, (ELEMS, LANES))
     for name in ("ahead", "geo", "back", "coef"):
         loads[name].wait()
-    for copy in exchange:
-        copy.wait_recv()
-    add_received(0, resid)
-
-    part_w[...] = operate(resid)
-    res0 = resid[...]
-    summing = start_sum(0, 0, dots(res0 * res0 * inv_mult[...], res0 * part_w[...]))
-    image[...] = part_w[...]
-    fill_send(1, image)
-    exchange = start_exchange(1)
-    summing = start_sum(0, 1, end_sum(0, 0, summing))
-    for copy in exchange:
-        copy.wait_recv()
-    add_received(1, image)
-
-    second[...] = operate(image)
-    fill_send(2, second)
-    exchange = start_exchange(2)
-    totals = end_sum(0, 1, summing)
+
+    @pl.loop(0, 2)
+    def _(turn):
+        for copy in exchange(turn):
+            copy.wait_recv()
+        add_received(turn, vec.at[turn])
+        terms = operate(vec.at[turn])
+        vec[turn + 1] = terms
+        parts[turn] = terms
+
+        @pl.when(turn == 0)
+        def _():
+            res0 = resid[...]
+            start_sum(0, 0, dots(res0 * res0 * inv_mult[...], res0 * parts[0]))
+
+        fill_send(turn + 1, vec.at[turn + 1])
+        for copy in exchange(turn + 1):
+            copy.start()
+
+        @pl.when(turn == 0)
+        def _():
+            start_sum(0, 1, end_sum(0, 0))
+
+    totals = end_sum(0, 1)
     norm0 = totals[:, 0:1]
     energy0 = totals[:, 1:2]
     alpha0 = norm0 / energy0
@@ -483,16 +499,18 @@
     image0 = image[...]
     res1 = res0 - alpha0 * image0
     scaled = res1 * inv_mult[...]
-    row = dots(scaled * res1, res1 * (part_w[...] - alpha0 * second[...]), scaled * image0)
-    summing = start_sum(1, 0, row)
-    for copy in exchange:
+    row = dots(scaled * res1, res1 * (parts[0] - alpha0 * parts[1]), scaled * image0)
+    start_sum(1, 0, row)
+    for copy in exchange(2):
         copy.wait_recv()
     add_received(2, second)
-    earlier = list(copies)
-    summing = start_sum(1, 1, end_sum(1, 0, summing))
-    for copy in earlier:
-        copy.wait_send()
-    totals = end_sum(1, 1, summing)
+    start_sum(1, 1, end_sum(1, 0))
+    for turn in range(3):
+        for copy in exchange(turn):
+            copy.wait_send()
+    for turn, stage in ((0, 0), (0, 1), (1, 0)):
+        sum_left(turn, stage)
+    totals = end_sum(1, 1)
     norm1 = totals[:, 0:1]
     beta = norm1 / norm0
     energy1 = totals[:, 1:2] + beta * (2.0 * totals[:, 2:3] + beta * energy0)
@@ -506,8 +524,7 @@
     left = res1 - alpha1 * image1
     sol_ref[...] = solved[0:ROWS]
     res_ref[...] = left[0:ROWS]
-    for copy in summing:
-        copy.wait_send()
+    sum_left(1, 1)
 
 
 def solution(mesh):
@@ -540,10 +557,8 @@
                 pltpu.VMEM(ahead.shape, jnp.float32),
                 pltpu.VMEM(back.shape, jnp.float32),
                 pltpu.VMEM((ELEMS, LANES), jnp.float32),
-                vector,
-                vector,
-                vector,
-                vector,
+                pltpu.VMEM((3, PAD, LANES), jnp.float32),
+                pltpu.VMEM((2, PAD, LANES), jnp.float32),
                 pltpu.VMEM((8 * ELEMS + 8, LANES), jnp.float32),
                 pltpu.VMEM((8 * ELEMS + 8, LANES), jnp.float32),
                 pltpu.VMEM((3, PAD, LANES), jnp.float32),
@@ -557,9 +572,9 @@
                 pltpu.VMEM((4 * FACE_ROWS + 8, LANES), jnp.int32),
                 pltpu.VMEM((4 * FACE_ROWS, LANES), jnp.int32),
                 pltpu.VMEM((8, 4 * LANES), jnp.int32),
-                pltpu.VMEM((3 * TURN, LANES), jnp.float32),
-                pltpu.VMEM((3 * TURN, LANES), jnp.float32),
-                pltpu.VMEM((3 * 32, LANES), jnp.float32),
+                pltpu.VMEM((3, TURN, LANES), jnp.float32),
+                pltpu.VMEM((3, TURN, LANES), jnp.float32),
+                pltpu.VMEM((3, 32, LANES), jnp.float32),
                 pltpu.VMEM((2 * (n_px + n_py), 1, LANES), jnp.float32),
                 pltpu.SemaphoreType.DMA((count,)),
                 pltpu.SemaphoreType.DMA((count,)),

time: 47.7 us -> 48.1 us (level)
  no operation moved by 1% of the time
where the time goes in v4:
time: 48.1 us; the launch traced here: 47.9 us
  Pallas kernels  45.2 us (94%)
  local copies, waits for them, and re-layouts  1.39 us (3%)
  between operations  1.29 us (3%)
    pallas_call x1, Pallas kernels, body(): pl.pallas_call(functools.partial(kernel, n_px, n_py), out_shape=(plane, p...  45.2 us
    reshape x2, local copies, waits for them, and re-layouts, body(): return (solved.reshape(shape), left.reshape(shape))  1.39 us

profile of v4, /device:TPU:1, one launch (start us, length us, event | category | flops | bytes accessed | tf_op | source)
XLA Modules:
  0.0 47.9 jit_solution(14587758541614558585)
XLA Ops:
  1.3 45.2 %shard_map.104 = (f32[129,128]{1,0:T(8,128)S(1)}, f32[129,128]{1,0:T(8,128)S(1)}) custom-call(f32[1,16512]{1,0:T(1,128)} %bitcast.7, f32[3,48,512]{2,1,0:T(8,128)} %bitcast.5, f32[1,48]{1,0:T(1,128)} %bitcast.9, s32[48,512]{1,0:T(8,128)} %bitcast.6, s32[1,1]{1,0:T(1,128)S(6)} %copy.11.count_ref, s32[4,1536]{1,0:T(4,128)} %bitcast.8, ...), custom_call_target="tpu_custom_call" | custom-call | flops 100000000 | bytes 2000000 | tf_op jit(solution)/shard_map/pallas_call | solution.py:545
  46.5 0.7 %reshape.10 = f32[1,1,16512]{2,1,0:T(1,128)} reshape(f32[129,128]{1,0:T(8,128)S(1)} %get-tuple-element.4) | data formatting | bytes 132096 | tf_op jit(solution)/shard_map/reshape | solution.py:601
  47.2 0.7 %reshape.11 = f32[1,1,16512]{2,1,0:T(1,128)} reshape(f32[129,128]{1,0:T(8,128)S(1)} %get-tuple-element.5) | data formatting | bytes 132096 | tf_op jit(solution)/shard_map/reshape | solution.py:601

commit v5 on v3

--- a/solution.py
+++ b/solution.py
@@ -17,6 +17,7 @@
 PAD = 136
 FACE_ROWS = FACE // LANES
 TURN = 80
+SCALE = 2.0**-16
 ROW_OF = [e * STRIDE // LANES for e in range(ELEMS)]
 LOWER = (1, 3, 2, 3)
 UPPER = (0, 2, 0, 1)
@@ -64,11 +65,11 @@
                 rows.append(matrix[2 * out + half, 2 * src + 1 - half])
         return np.stack(rows)
 
-    coef = np.concatenate([lanes_of(deriv), lanes_of(deriv.T)])
+    coef = np.concatenate([lanes_of(deriv), SCALE * lanes_of(deriv.T)])
     second = np.kron(np.eye(2), np.kron(deriv, np.eye(8)))
     third = np.kron(np.eye(16), deriv)
     ahead = np.concatenate([second.T, third.T], axis=1)
-    back = np.concatenate([second, third], axis=0)
+    back = SCALE * np.concatenate([second, third], axis=0)
     return tuple(np.asarray(t, np.float32) for t in (coef, ahead, back))
 
 
@@ -84,6 +85,36 @@
         found = take_lanes(source, lanes)
         total = jnp.where(high == j, found, 0.0 if total is None else total)
     return total
+
+
+def sum_exactly(rows):
+    errors = []
+    while len(rows) > 1:
+        sums_of = []
+        for x, y in zip(rows[::2], rows[1::2]):
+            total = x + y
+            part = total - x
+            errors.append((x - (total - part)) + (y - part))
+            sums_of.append(total)
+        rows = sums_of
+    while len(errors) > 1:
+        odd = errors[len(errors) // 2 * 2 :]
+        errors = [x + y for x, y in zip(errors[::2], errors[1::2])] + odd
+    return rows[0], errors[0]
+
+
+def split(x):
+    small = x * 2.0**-16
+    wide = small * 4097.0
+    high = (wide - (wide - small)) * 2.0**16
+    return high, x - high
+
+
+def product_less(factor, times, less):
+    product = factor * times[0]
+    (f_high, f_low), (t_high, t_low) = split(factor), split(times[0])
+    error = ((f_high * t_high - product) + f_high * t_low + f_low * t_high) + f_low * t_low
+    return (product - less[0]) + ((error - less[1]) + factor * times[1])
 
 
 def eight(row):
@@ -141,7 +172,7 @@
     resid,
     image,
     second,
-    part_w,
+    part,
     windows,
     spread,
     sums,
@@ -239,20 +270,15 @@
             )
         return started
 
-    def start_sum(turn, stage, row):
-        first = turn * (n_px + n_py) + stage * n_px
-        mine = first + place(stage)
+    def start_sum(stage, row):
+        mine = stage * n_px + place(stage)
         red[pl.ds(mine, 1)] = row[None]
         return [start_copy(red.at[mine], red.at[mine], other) for other in partners(stage)]
 
-    def end_sum(turn, stage, started):
-        first = turn * (n_px + n_py) + stage * n_px
+    def end_sum(stage, started):
         for copy in started:
             copy.wait_recv()
-        sums_of = [red[first + slot] for slot in range(sizes[stage])]
-        while len(sums_of) > 1:
-            sums_of = [x + y for x, y in zip(sums_of[::2], sums_of[1::2])]
-        return sums_of[0]
+        return sum_exactly([red[stage * n_px + slot] for slot in range(sizes[stage])])
 
     live = count_ref[...]
 
@@ -414,10 +440,10 @@
         sums[0, 0:8, :] += pick([eight(last_row(r)) for r in result], wrap_inv[...])
         return sums[0] + sums[1] + sums[2]
 
-    def dots(*products):
-        lane = iota((1, LANES), 1)
-        row = jnp.zeros((1, LANES), jnp.float32)
-        for k, product in enumerate(products):
+    lane = iota((1, LANES), 1)
+
+    def dots(first, row, *products):
+        for k, product in enumerate(products, first):
             total = jnp.sum(jnp.sum(product, axis=0, keepdims=True), axis=1, keepdims=True)
             row = jnp.where(lane == k, total, row)
         return row
@@ -453,56 +479,59 @@
     set_up()
     same = iota((ELEMS, ELEMS), 0) == iota((ELEMS, ELEMS), 1)
     column = jnp.sum(jnp.where(same, shift_ref[...], 0.0), axis=1, keepdims=True)
-    factors[...] = jnp.broadcast_to(column, (ELEMS, LANES))
+    factors[...] = jnp.broadcast_to(SCALE * column, (ELEMS, LANES))
     for name in ("ahead", "geo", "back", "coef"):
         loads[name].wait()
     for copy in exchange:
         copy.wait_recv()
     add_received(0, resid)
 
-    part_w[...] = operate(resid)
-    res0 = resid[...]
-    summing = start_sum(0, 0, dots(res0 * res0 * inv_mult[...], res0 * part_w[...]))
-    image[...] = part_w[...]
+    part[...] = operate(resid)
+    image[...] = part[...]
     fill_send(1, image)
     exchange = start_exchange(1)
-    summing = start_sum(0, 1, end_sum(0, 0, summing))
+    res0 = resid[...]
+    row = jnp.zeros((1, LANES), jnp.float32)
+    row = dots(0, row, res0 * res0 * inv_mult[...], res0 * part[...])
     for copy in exchange:
         copy.wait_recv()
     add_received(1, image)
 
-    second[...] = operate(image)
+    part[...] = operate(image)
+    image0 = image[...]
+    row = dots(2, row, image0 * image0 * inv_mult[...], image0 * part[...])
+    summing = start_sum(0, row)
+    second[...] = part[...]
     fill_send(2, second)
     exchange = start_exchange(2)
-    totals = end_sum(0, 1, summing)
-    norm0 = totals[:, 0:1]
-    energy0 = totals[:, 1:2]
-    alpha0 = norm0 / energy0
-
-    res0 = resid[...]
-    image0 = image[...]
-    res1 = res0 - alpha0 * image0
-    scaled = res1 * inv_mult[...]
-    row = dots(scaled * res1, res1 * (part_w[...] - alpha0 * second[...]), scaled * image0)
-    summing = start_sum(1, 0, row)
+    total, rest = end_sum(0, summing)
+    summing = start_sum(1, jnp.where(lane < 64, total, pltpu.roll(rest, 64, 1)))
     for copy in exchange:
         copy.wait_recv()
     add_received(2, second)
-    earlier = list(copies)
-    summing = start_sum(1, 1, end_sum(1, 0, summing))
-    for copy in earlier:
+    for copy in copies[: -len(summing)]:
         copy.wait_send()
-    totals = end_sum(1, 1, summing)
-    norm1 = totals[:, 0:1]
-    beta = norm1 / norm0
-    energy1 = totals[:, 1:2] + beta * (2.0 * totals[:, 2:3] + beta * energy0)
+    total, rest = end_sum(1, summing)
+    rest = rest + pltpu.roll(total, 64, 1)
+
+    def scalar(k):
+        return total[:, k : k + 1], rest[:, k : k + 1]
+
+    norm0, energy0, square, bend = (scalar(k) for k in range(4))
+    alpha0 = norm0[0] / energy0[0]
+    lack = product_less(alpha0, energy0, norm0)
+    excess = product_less(alpha0, square, energy0)
+    curve = product_less(alpha0, bend, square)
+    norm1 = alpha0 * excess - lack
+    beta = norm1 / norm0[0]
+    energy1 = (alpha0 * curve - excess) + beta * (beta * energy0[0] - 2.0 * excess)
     alpha1 = norm1 / energy1
 
     res0 = resid[...]
     image0 = image[...]
     res1 = res0 - alpha0 * image0
     image1 = (image0 - alpha0 * second[...]) + beta * image0
-    solved = alpha0 * res0 + alpha1 * (res1 + beta * res0)
+    solved = (SCALE * alpha0) * res0 + (SCALE * alpha1) * (res1 + beta * res0)
     left = res1 - alpha1 * image1
     sol_ref[...] = solved[0:ROWS]
     res_ref[...] = left[0:ROWS]
@@ -513,7 +542,7 @@
 def solution(mesh):
     n_px = mesh.shape["px"]
     n_py = mesh.shape["py"]
-    count = 3 * 8 + 2 * (n_px - 1 + n_py - 1)
+    count = 3 * 8 + (n_px - 1 + n_py - 1)
     coef, ahead, back = tables()
 
     def body(right_side, geometry, shift, node_order, elem_counts, share_lists):
@@ -560,7 +589,7 @@
                 pltpu.VMEM((3 * TURN, LANES), jnp.float32),
                 pltpu.VMEM((3 * TURN, LANES), jnp.float32),
                 pltpu.VMEM((3 * 32, LANES), jnp.float32),
-                pltpu.VMEM((2 * (n_px + n_py), 1, LANES), jnp.float32),
+                pltpu.VMEM((n_px + n_py, 1, LANES), jnp.float32),
                 pltpu.SemaphoreType.DMA((count,)),
                 pltpu.SemaphoreType.DMA((count,)),
                 pltpu.SemaphoreType.DMA((8,)),

time: 47.7 us -> 43.5 us (0.912)
  Pallas kernels: 44.8 us -> 40.7 us
    pallas_call x1, Pallas kernels: 44.8 us -> 40.7 us  [body(): pl.pallas_call(functools.partial(kernel, n_px, n_py), out_shape=(plane, p...]
where the time goes in v5:
time: 43.5 us; the launch traced here: 43.4 us
  Pallas kernels  40.7 us (94%)
  local copies, waits for them, and re-layouts  1.39 us (3%)
  between operations  1.29 us (3%)
    pallas_call x1, Pallas kernels, body(): pl.pallas_call(functools.partial(kernel, n_px, n_py), out_shape=(plane, p...  40.7 us
    reshape x2, local copies, waits for them, and re-layouts, body(): return (solved.reshape(shape), left.reshape(shape))  1.39 us

profile of v5, /device:TPU:1, one launch (start us, length us, event | category | flops | bytes accessed | tf_op | source)
XLA Modules:
  0.0 43.4 jit_solution(12600868148827657539)
XLA Ops:
  1.3 40.7 %shard_map.104 = (f32[129,128]{1,0:T(8,128)S(1)}, f32[129,128]{1,0:T(8,128)S(1)}) custom-call(f32[1,16512]{1,0:T(1,128)} %bitcast.7, f32[3,48,512]{2,1,0:T(8,128)} %bitcast.5, f32[1,48]{1,0:T(1,128)} %bitcast.9, s32[48,512]{1,0:T(8,128)} %bitcast.6, s32[1,1]{1,0:T(1,128)S(6)} %copy.11.count_ref, s32[4,1536]{1,0:T(4,128)} %bitcast.8, ...), custom_call_target="tpu_custom_call" | custom-call | flops 100000000 | bytes 2000000 | tf_op jit(solution)/shard_map/pallas_call | solution.py:557
  42.0 0.7 %reshape.10 = f32[1,1,16512]{2,1,0:T(1,128)} reshape(f32[129,128]{1,0:T(8,128)S(1)} %get-tuple-element.4) | data formatting | bytes 132096 | tf_op jit(solution)/shard_map/reshape | solution.py:615
  42.7 0.7 %reshape.11 = f32[1,1,16512]{2,1,0:T(1,128)} reshape(f32[129,128]{1,0:T(8,128)S(1)} %get-tuple-element.5) | data formatting | bytes 132096 | tf_op jit(solution)/shard_map/reshape | solution.py:615

commit v6 on v5

--- a/solution.py
+++ b/solution.py
@@ -125,8 +125,21 @@
     return lax.broadcasted_iota(jnp.int32, shape, dim)
 
 
-def one_hot_lanes(low):
-    return jnp.where(low == iota((LANES, low.shape[1]), 0), 1.0, 0.0).astype(jnp.bfloat16)
+def as_bf16(values):
+    return values.astype(jnp.float32).astype(jnp.bfloat16)
+
+
+def one_hot_lanes(low, row_number):
+    low = as_bf16(low)
+    one = jnp.ones((LANES, LANES), jnp.bfloat16)
+    zero = jnp.zeros((LANES, LANES), jnp.bfloat16)
+    return jnp.concatenate(
+        [
+            jnp.where(row_number == low[:, at : at + LANES], one, zero)
+            for at in range(0, low.shape[1], LANES)
+        ],
+        axis=1,
+    )
 
 
 def over_lanes(left, right):
@@ -135,14 +148,14 @@
     )
 
 
-def inverse_rows(high, low, groups):
+def inverse_rows(high, low, groups, row_number):
     count = high.shape[1]
     number = iota((groups, count), 1) + 1
     hit = high == iota((groups, count), 0)
     tens = jnp.where(hit, number >> 4, 0).astype(jnp.float32)
     ones = jnp.where(hit, number & 15, 0).astype(jnp.float32)
     left = jnp.concatenate([tens, ones], axis=0).astype(jnp.bfloat16)
-    found = over_lanes(left, one_hot_lanes(low))
+    found = over_lanes(left, one_hot_lanes(low, row_number))
     return (16.0 * found[:groups] + found[groups:]).astype(jnp.int32) - 1
 
 
@@ -221,10 +234,13 @@
     def place(stage):
         return px if stage == 0 else py
 
+    def far_first(size):
+        return sorted(range(1, size), key=lambda d: (-min(d, size - d), d))
+
     def partners(stage):
         if stage == 0:
-            return [(lax.rem(px + d, n_px), py) for d in range(1, n_px)]
-        return [(px, lax.rem(py + d, n_py)) for d in range(1, n_py)]
+            return [(lax.rem(px + d, n_px), py) for d in far_first(n_px)]
+        return [(px, lax.rem(py + d, n_py)) for d in far_first(n_py)]
 
     everyone = [moved(*step) for step in FACE_STEPS + DIAG_STEPS]
     everyone += partners(0) + partners(1)
@@ -335,14 +351,15 @@
         return jnp.sum(jnp.where(is_last, values, jnp.zeros_like(values)), axis=0, keepdims=True)
 
     def set_up():
+        row_number = as_bf16(iota((LANES, LANES), 0))
         for f in range(4):
             row = lists_ref[f : f + 1, 0:FACE]
-            face_inv[16 * f : 16 * f + 16, :] = inverse_rows(row >> 7, row & 127, 16)
+            face_inv[16 * f : 16 * f + 16, :] = inverse_rows(row >> 7, row & 127, 16, row_number)
             for part in range(2):
                 at = FACE + part * DIAG
                 row = lists_ref[f : f + 1, at : at + DIAG]
                 number = (iota((8, DIAG), 1) + 1).astype(jnp.float32).astype(jnp.bfloat16)
-                found = over_lanes(number, one_hot_lanes(row))
+                found = over_lanes(number, one_hot_lanes(row, row_number))
                 cross_inv[4 * part + f : 4 * part + f + 1, :] = found[0:1].astype(jnp.int32) - 1
         for i in range(half):
             pair_up(
@@ -365,21 +382,21 @@
             at = 4 * FACE_ROWS + q
             inv_mult[at : at + 1, :] = 1.0 / copies_of
 
-        @pl.loop(0, ELEMS // 8)
+        @pl.loop(0, ELEMS // 16)
         def _(group):
-            block = order_ref[pl.ds(pl.multiple_of(8 * group, 8), 8), :]
-            for s in range(8):
-                e = 8 * group + s
+            block = order_ref[pl.ds(pl.multiple_of(16 * group, 16), 16), :]
+            for s in range(16):
+                e = 16 * group + s
                 row = block[s : s + 1]
-                shifted = row + lax.rem(e * STRIDE, LANES)
+                shifted = row + s * STRIDE % LANES
                 own = jnp.where(live <= e, 0, jnp.where(live == e + 1, STRIDE, 4 * LANES))
                 high = jnp.where(row >= own, 7, shifted >> 7)
                 elem_inv[pl.ds(pl.multiple_of(8 * e, 8), 8), :] = inverse_rows(
-                    high, shifted & 127, 8
+                    high, shifted & 127, 8, row_number
                 )
 
         wrapped = jnp.concatenate([last_row(orders(c)) for c in range(4)], axis=1) - STRIDE
-        wrap_inv[...] = inverse_rows(wrapped >> 7, wrapped & 127, 8)
+        wrap_inv[...] = inverse_rows(wrapped >> 7, wrapped & 127, 8, row_number)
         wrap_idx[...] = eight(wrapped)
 
     def derivative(chunks, first):

time: 43.5 us -> 43.4 us (level)
  no operation moved by 1% of the time
where the time goes in v6:
time: 43.4 us; the launch traced here: 43.2 us
  Pallas kernels  40.5 us (93%)
  local copies, waits for them, and re-layouts  1.39 us (3%)
  between operations  1.29 us (3%)
    pallas_call x1, Pallas kernels, body(): pl.pallas_call(functools.partial(kernel, n_px, n_py), out_shape=(plane, p...  40.5 us
    reshape x2, local copies, waits for them, and re-layouts, body(): return (solved.reshape(shape), left.reshape(shape))  1.39 us

profile of v6, /device:TPU:1, one launch (start us, length us, event | category | flops | bytes accessed | tf_op | source)
XLA Modules:
  0.0 43.2 jit_solution(5383564962378736187)
XLA Ops:
  1.3 40.5 %shard_map.104 = (f32[129,128]{1,0:T(8,128)S(1)}, f32[129,128]{1,0:T(8,128)S(1)}) custom-call(f32[1,16512]{1,0:T(1,128)} %bitcast.7, f32[3,48,512]{2,1,0:T(8,128)} %bitcast.5, f32[1,48]{1,0:T(1,128)} %bitcast.9, s32[48,512]{1,0:T(8,128)} %bitcast.6, s32[1,1]{1,0:T(1,128)S(6)} %copy.11.count_ref, s32[4,1536]{1,0:T(4,128)} %bitcast.8, ...), custom_call_target="tpu_custom_call" | custom-call | flops 100000000 | bytes 2000000 | tf_op jit(solution)/shard_map/pallas_call | solution.py:574
  41.8 0.7 %reshape.10 = f32[1,1,16512]{2,1,0:T(1,128)} reshape(f32[129,128]{1,0:T(8,128)S(1)} %get-tuple-element.4) | data formatting | bytes 132096 | tf_op jit(solution)/shard_map/reshape | solution.py:632
  42.5 0.7 %reshape.11 = f32[1,1,16512]{2,1,0:T(1,128)} reshape(f32[129,128]{1,0:T(8,128)S(1)} %get-tuple-element.5) | data formatting | bytes 132096 | tf_op jit(solution)/shard_map/reshape | solution.py:632

commit v7 on v6

--- a/solution.py
+++ b/solution.py
@@ -70,7 +70,31 @@
     third = np.kron(np.eye(16), deriv)
     ahead = np.concatenate([second.T, third.T], axis=1)
     back = SCALE * np.concatenate([second, third], axis=0)
-    return tuple(np.asarray(t, np.float32) for t in (coef, ahead, back))
+    halves = [ahead[:, :LANES], ahead[:, LANES:], back]
+    parts = np.concatenate([part for half in halves for part in three_parts(half)], axis=0)
+    return np.asarray(coef, np.float32), parts
+
+
+def three_parts(table):
+    rest = np.asarray(table, np.float32)
+    parts = []
+    for _ in range(3):
+        part = rest.astype(jnp.bfloat16)
+        parts.append(part)
+        rest = rest - part.astype(np.float32)
+    return parts
+
+
+def three_ways(values):
+    first = values.astype(jnp.bfloat16)
+    rest = values - first.astype(jnp.float32)
+    second = rest.astype(jnp.bfloat16)
+    return first, second, (rest - second.astype(jnp.float32)).astype(jnp.bfloat16)
+
+
+def product(pieces, table):
+    left = jnp.concatenate(pieces, axis=1)
+    return jnp.dot(left, table, preferred_element_type=jnp.float32)
 
 
 def take_lanes(values, lanes):
@@ -169,8 +193,7 @@
     count_ref,
     lists_hbm,
     coef_hbm,
-    ahead_hbm,
-    back_hbm,
+    parts_hbm,
     sol_ref,
     res_ref,
     rhs_ref,
@@ -179,8 +202,7 @@
     order_ref,
     lists_ref,
     coef_ref,
-    ahead_ref,
-    back_ref,
+    parts_ref,
     factors,
     resid,
     image,
@@ -214,9 +236,8 @@
             ("rhs", rhs_hbm, rhs_ref),
             ("order", order_hbm, order_ref),
             ("shift", shift_hbm, shift_ref),
-            ("ahead", ahead_hbm, ahead_ref),
+            ("parts", parts_hbm, parts_ref),
             ("geo", geo_hbm, geo_ref),
-            ("back", back_hbm, back_ref),
             ("coef", coef_hbm, coef_ref),
         )
     ):
@@ -430,17 +451,27 @@
             )[0:1]
             values = pick(rows, order + offset)
             chunks.append(jnp.where(is_last & (order >= STRIDE), around, values))
-        exact = lax.Precision.HIGHEST
-        narrow = jnp.concatenate(chunks, axis=0)
-        grads = jnp.dot(
-            narrow, ahead_ref[...], precision=exact, preferred_element_type=jnp.float32
-        )
+        a1, a2, a3 = (
+            jnp.concatenate(
+                [parts_ref[at : at + LANES, :] for at in (k * LANES, (3 + k) * LANES)], axis=1
+            )
+            for k in range(3)
+        )
+        ahead = jnp.concatenate([a1, a1, a2, a2, a1, a3], axis=0)
+        b1, b2, b3 = (
+            parts_ref[(6 + 2 * k) * LANES : (8 + 2 * k) * LANES, :] for k in range(3)
+        )
+        back_wide = jnp.concatenate([b1, b2], axis=1)
+        back_wide = jnp.concatenate([back_wide, back_wide], axis=0)
+        back_rest = jnp.concatenate([b1, b3], axis=0)
+        u1, u2, u3 = three_ways(jnp.concatenate(chunks, axis=0))
+        grads = product([u1, u2, u1, u2, u3, u1], ahead)
         fluxes = jnp.concatenate(
             [stacked(1) * grads[:, :LANES], stacked(2) * grads[:, LANES:]], axis=1
         )
-        terms = jnp.dot(
-            fluxes, back_ref[...], precision=exact, preferred_element_type=jnp.float32
-        )
+        u1, u2, u3 = three_ways(fluxes)
+        wide = product([u1, u2], back_wide)
+        terms = product([u3, u1], back_rest) + wide[:, LANES:] + wide[:, :LANES]
         grad = derivative(chunks, 0)
         grad = [geo_ref[0, :, c * LANES : (c + 1) * LANES] * grad[c] for c in range(4)]
         first = derivative(grad, 32)
@@ -497,7 +528,7 @@
     same = iota((ELEMS, ELEMS), 0) == iota((ELEMS, ELEMS), 1)
     column = jnp.sum(jnp.where(same, shift_ref[...], 0.0), axis=1, keepdims=True)
     factors[...] = jnp.broadcast_to(SCALE * column, (ELEMS, LANES))
-    for name in ("ahead", "geo", "back", "coef"):
+    for name in ("parts", "geo", "coef"):
         loads[name].wait()
     for copy in exchange:
         copy.wait_recv()
@@ -560,7 +591,7 @@
     n_px = mesh.shape["px"]
     n_py = mesh.shape["py"]
     count = 3 * 8 + (n_px - 1 + n_py - 1)
-    coef, ahead, back = tables()
+    coef, parts = tables()
 
     def body(right_side, geometry, shift, node_order, elem_counts, share_lists):
         vmem = pl.BlockSpec(memory_space=pltpu.VMEM)
@@ -574,7 +605,7 @@
         solved, left = pl.pallas_call(
             functools.partial(kernel, n_px, n_py),
             out_shape=(plane, plane),
-            in_specs=[hbm] * 4 + [vmem] + [hbm] * 4,
+            in_specs=[hbm] * 4 + [vmem] + [hbm] * 3,
             out_specs=(vmem, vmem),
             scratch_shapes=[
                 pltpu.VMEM((1, ROWS * LANES), jnp.float32),
@@ -583,8 +614,7 @@
                 pltpu.VMEM((ELEMS, 4 * LANES), jnp.int32),
                 pltpu.VMEM((4, FACE + 2 * DIAG), jnp.int32),
                 pltpu.VMEM(coef.shape, jnp.float32),
-                pltpu.VMEM(ahead.shape, jnp.float32),
-                pltpu.VMEM(back.shape, jnp.float32),
+                pltpu.VMEM(parts.shape, jnp.bfloat16),
                 pltpu.VMEM((ELEMS, LANES), jnp.float32),
                 vector,
                 vector,
@@ -609,7 +639,7 @@
                 pltpu.VMEM((n_px + n_py, 1, LANES), jnp.float32),
                 pltpu.SemaphoreType.DMA((count,)),
                 pltpu.SemaphoreType.DMA((count,)),
-                pltpu.SemaphoreType.DMA((8,)),
+                pltpu.SemaphoreType.DMA((7,)),
             ],
             compiler_params=pltpu.CompilerParams(
                 collective_id=0, has_side_effects=True, vmem_limit_bytes=32 * 2**20
@@ -625,8 +655,7 @@
             elem_counts,
             stay(share_lists[0, 0]),
             stay(jnp.asarray(coef)),
-            stay(jnp.asarray(ahead)),
-            stay(jnp.asarray(back)),
+            stay(jnp.asarray(parts)),
         )
         shape = (1, 1, ROWS * LANES)
         return solved.reshape(shape), left.reshape(shape)

time: 43.4 us -> 42.9 us (0.988)
    pallas_call x1, Pallas kernels: 40.5 us -> 40.1 us  [body(): pl.pallas_call(functools.partial(kernel, n_px, n_py), out_shape=(plane, p...]
where the time goes in v7:
time: 42.9 us; the launch traced here: 42.8 us
  Pallas kernels  40.1 us (93%)
  local copies, waits for them, and re-layouts  1.39 us (3%)
  between operations  1.29 us (3%)
    pallas_call x1, Pallas kernels, body(): pl.pallas_call(functools.partial(kernel, n_px, n_py), out_shape=(plane, p...  40.1 us
    reshape x2, local copies, waits for them, and re-layouts, body(): return (solved.reshape(shape), left.reshape(shape))  1.39 us

profile of v7, /device:TPU:1, one launch (start us, length us, event | category | flops | bytes accessed | tf_op | source)
XLA Modules:
  0.0 42.8 jit_solution(4801156818891951589)
XLA Ops:
  1.3 40.1 %shard_map.95 = (f32[129,128]{1,0:T(8,128)S(1)}, f32[129,128]{1,0:T(8,128)S(1)}) custom-call(f32[1,16512]{1,0:T(1,128)} %bitcast.7, f32[3,48,512]{2,1,0:T(8,128)} %bitcast.5, f32[1,48]{1,0:T(1,128)} %bitcast.9, s32[48,512]{1,0:T(8,128)} %bitcast.6, s32[1,1]{1,0:T(1,128)S(6)} %copy.10.count_ref, s32[4,1536]{1,0:T(4,128)} %bitcast.8, ...), custom_call_target="tpu_custom_call" | custom-call | flops 100000000 | bytes 2000000 | tf_op jit(solution)/shard_map/pallas_call | solution.py:605
  41.4 0.7 %reshape.10 = f32[1,1,16512]{2,1,0:T(1,128)} reshape(f32[129,128]{1,0:T(8,128)S(1)} %get-tuple-element.4) | data formatting | bytes 132096 | tf_op jit(solution)/shard_map/reshape | solution.py:661
  42.1 0.7 %reshape.11 = f32[1,1,16512]{2,1,0:T(1,128)} reshape(f32[129,128]{1,0:T(8,128)S(1)} %get-tuple-element.5) | data formatting | bytes 132096 | tf_op jit(solution)/shard_map/reshape | solution.py:661

commit v8 on v7

--- a/solution.py
+++ b/solution.py
@@ -581,8 +581,9 @@
     image1 = (image0 - alpha0 * second[...]) + beta * image0
     solved = (SCALE * alpha0) * res0 + (SCALE * alpha1) * (res1 + beta * res0)
     left = res1 - alpha1 * image1
-    sol_ref[...] = solved[0:ROWS]
-    res_ref[...] = left[0:ROWS]
+    for i in range(ROWS):
+        sol_ref[:, i * LANES : (i + 1) * LANES] = solved[i : i + 1]
+        res_ref[:, i * LANES : (i + 1) * LANES] = left[i : i + 1]
     for copy in summing:
         copy.wait_send()
 
@@ -596,7 +597,7 @@
     def body(right_side, geometry, shift, node_order, elem_counts, share_lists):
         vmem = pl.BlockSpec(memory_space=pltpu.VMEM)
         hbm = pl.BlockSpec(memory_space=pltpu.HBM)
-        plane = jax.ShapeDtypeStruct((ROWS, LANES), jnp.float32)
+        plane = jax.ShapeDtypeStruct((1, ROWS * LANES), jnp.float32)
 
         def stay(x):
             return pltpu.with_memory_space_constraint(x, pltpu.HBM)

time: 42.9 us -> 42.9 us (level)
    reshape x2 -> x0, local copies, waits for them, and re-layouts: 1.39 us -> none  [body(): return (solved.reshape(shape), left.reshape(shape))]
    unnamed x0 -> x2, local copies, waits for them, and re-layouts: none -> 1.26 us
where the time goes in v8:
time: 42.9 us; the launch traced here: 42.7 us
  Pallas kernels  40.2 us (94%)
  between operations  1.29 us (3%)
  local copies, waits for them, and re-layouts  1.26 us (3%)
    pallas_call x1, Pallas kernels, body(): pl.pallas_call(functools.partial(kernel, n_px, n_py), out_shape=(plane, p...  40.2 us
    unnamed x2, local copies, waits for them, and re-layouts  1.26 us

profile of v8, /device:TPU:1, one launch (start us, length us, event | category | flops | bytes accessed | tf_op | source)
XLA Modules:
  0.0 42.7 jit_solution(2755906087114375268)
XLA Ops:
  1.3 40.2 %shard_map.95 = (f32[1,16512]{1,0:T(1,128)S(1)}, f32[1,16512]{1,0:T(1,128)S(1)}) custom-call(f32[1,16512]{1,0:T(1,128)} %bitcast.11, f32[3,48,512]{2,1,0:T(8,128)} %bitcast.9, f32[1,48]{1,0:T(1,128)} %bitcast.13, s32[48,512]{1,0:T(8,128)} %bitcast.10, s32[1,1]{1,0:T(1,128)S(6)} %copy.12.count_ref, s32[4,1536]{1,0:T(4,128)} %bitcast.12, ...), custom_call_target="tpu_custom_call" | custom-call | flops 100000000 | bytes 2000000 | tf_op jit(solution)/shard_map/pallas_call | solution.py:606
  41.5 0.6 %copy.13 = f32[1,1,16512]{2,1,0:T(1,128)} copy(f32[1,1,16512]{2,1,0:T(1,128)S(1)} %bitcast.8) | data formatting | bytes 132096
  42.1 0.6 %copy.14 = f32[1,1,16512]{2,1,0:T(1,128)} copy(f32[1,1,16512]{2,1,0:T(1,128)S(1)} %bitcast.7) | data formatting | bytes 132096
